TPU v7x, 32 devices: a whole 2x2x4 slice. The times are simulated.
32 devices in a mesh: gx: 4 (over y, x), gy: 8 (over z, core).
Axes of the slice: x: 2, y: 2, z: 4, core: 2. Of those that a mesh axis runs over, the one named last changes fastest.
Arguments:
- velocity: bfloat16 [3, 64, 256, 256], P(None, 'gx', 'gy'), may hold values from -4 to 4
- density: bfloat16 [64, 256, 256], P('gx', 'gy'), may hold values from 0 to 1
Outputs:
- projected: float32 [3, 64, 256, 256], P(None, 'gx', 'gy')
- emission: float32 [64, 256, 256], P('gx', 'gy')
All inputs are finite; a program needn't handle non-finite values.
Results may differ from a plain program's by a relative error of at most 0.0003.
Values sent between devices are 32-bit elements; how exact they have to be, the bound alone decides.
A program may use at most 64 MiB of HBM per device.

v0:
```python
import jax
import jax.numpy as jnp
from jax import lax
from jax.sharding import PartitionSpec as P

time_step = 0.4
buoyancy = 2.0
extinction = 3.0
highest = lax.Precision.HIGHEST


def padded_2(block, sides, width):
    for axis, dim in sides:
        count = lax.axis_size(axis)
        forward = [(i, i + 1) for i in range(count - 1)]
        backward = [(target, source) for source, target in forward]
        low = lax.ppermute(
            lax.slice_in_dim(block, block.shape[dim] - width, None, axis=dim), axis, forward
        )
        high = lax.ppermute(lax.slice_in_dim(block, 0, width, axis=dim), axis, backward)
        block = jnp.concatenate([low, block, high], axis=dim)
    return block


def entering(part, axis, combine, identity):
    place = lax.axis_index(axis)
    gathered = lax.all_gather(part, axis)
    state = jnp.zeros_like(part) + jnp.asarray(identity, part.dtype)

    def one(turn, state):
        return combine(state, lax.dynamic_index_in_dim(gathered, turn, 0, False))

    return lax.fori_loop(0, place, one, state)


def cosine_table(length):
    modes = jnp.arange(length, dtype=jnp.float32)[:, None]
    centres = jnp.arange(length, dtype=jnp.float32)[None, :] + 0.5
    factor = jnp.where(modes == 0, jnp.sqrt(1.0 / length), jnp.sqrt(2.0 / length))
    return factor * jnp.cos(jnp.pi * modes * centres / length)


def flux_terms(padded):
    extent = padded.shape

    def window(offset_x, offset_y, offset_z):
        return padded[
            :,
            2 + offset_x : extent[1] - 2 + offset_x,
            2 + offset_y : extent[2] - 2 + offset_y,
            2 + offset_z : extent[3] - 2 + offset_z,
        ]

    def moved(axis_id, offset):
        offsets = [0, 0, 0]
        offsets[axis_id] = offset
        return window(offsets[0], offsets[1], offsets[2])

    middle = window(0, 0, 0)
    summed = jnp.zeros_like(middle)
    for axis_id in range(3):
        plus_one = moved(axis_id, 1)
        plus_two = moved(axis_id, 2)
        minus_one = moved(axis_id, -1)
        minus_two = moved(axis_id, -2)
        lower_diff = (2.0 * plus_one + 3.0 * middle - 6.0 * minus_one + minus_two) / 6.0
        upper_diff = (-plus_two + 6.0 * plus_one - 3.0 * middle - 2.0 * minus_one) / 6.0
        speed_axis = middle[axis_id]
        summed = (
            summed
            + jnp.maximum(speed_axis, 0.0) * lower_diff
            + jnp.minimum(speed_axis, 0.0) * upper_diff
        )
    return -summed


def tendency_rim(extended):
    return flux_terms(jnp.pad(extended, ((0, 0), (0, 0), (0, 0), (2, 2))))


def cropped(extended, have_rim, want_rim):
    cut_size = have_rim - want_rim
    return extended[
        :, cut_size : extended.shape[1] - cut_size, cut_size : extended.shape[2] - cut_size, :
    ]


def advect_halo(fields, rim_width):
    return padded_2(fields, (("gx", 1), ("gy", 2)), rim_width)


def eigen_row(modes, length):
    return 2.0 - 2.0 * jnp.cos(jnp.pi * modes / length)


def per_device(velocity, density):
    block_x, block_y, length_z = density.shape
    count_x = lax.axis_size("gx")
    count_y = lax.axis_size("gy")
    full_x = block_x * count_x
    full_y = block_y * count_y
    anchor_x = lax.axis_index("gx") * block_x
    anchor_y = lax.axis_index("gy") * block_y
    layers = length_z // (count_x * count_y)

    def confine(fields, rim_width):
        along_x = anchor_x - rim_width + jnp.arange(block_x + 2 * rim_width)
        along_y = anchor_y - rim_width + jnp.arange(block_y + 2 * rim_width)
        along_z = jnp.arange(length_z)
        inside = ((along_x >= 0) & (along_x < full_x))[:, None, None] & (
            (along_y >= 0) & (along_y < full_y)
        )[None, :, None]
        open_x = inside & (along_x < full_x - 1)[:, None, None]
        open_y = inside & (along_y < full_y - 1)[None, :, None]
        open_z = inside & (along_z < length_z - 1)[None, None, :]
        return jnp.stack(
            [fields[0] * open_x, fields[1] * open_y, fields[2] * open_z, fields[3] * inside]
        )

    fields = jnp.concatenate(
        [velocity.astype(jnp.float32), density.astype(jnp.float32)[None]], axis=0
    )
    widened = advect_halo(fields, 2)
    section_one = confine(fields + time_step * tendency_rim(widened), 0)
    section_one = advect_halo(section_one, 3)
    earlier = cropped(widened, 2, 1)
    section_two = confine(
        0.5 * earlier + 0.5 * (cropped(section_one, 3, 1) + time_step * tendency_rim(section_one)),
        1,
    )
    smoke_now = section_two[3]
    smoke_above = jnp.concatenate(
        [smoke_now[:, :, 1:], jnp.zeros_like(smoke_now[:, :, :1])], axis=2
    )
    lifted = confine(
        jnp.stack(
            [
                section_two[0],
                section_two[1],
                section_two[2] + time_step * buoyancy * 0.5 * (smoke_now + smoke_above),
                smoke_now,
            ]
        ),
        1,
    )
    interior = lifted[:, 1:-1, 1:-1, :]
    below_z = jnp.concatenate(
        [jnp.zeros_like(interior[2][:, :, :1]), interior[2][:, :, :-1]], axis=2
    )
    divergence = (
        interior[0]
        - lifted[0, :-2, 1:-1, :]
        + (interior[1] - lifted[1, 1:-1, :-2, :])
        + (interior[2] - below_z)
    )
    column = interior[3]
    attenuation = extinction / full_x
    running = jnp.cumsum(column, axis=0)
    before = entering(running[-1], "gx", jnp.add, jnp.zeros_like(running[-1]))
    optical = attenuation * (before[None] + running - column)
    emission = jnp.exp(-optical) * -jnp.expm1(-attenuation * column) / attenuation
    table_z = cosine_table(length_z)
    table_x = cosine_table(full_x)
    table_y = cosine_table(full_y)
    along_kz = jnp.einsum("xyn,kn->kxy", divergence, table_z, precision=highest)
    planes = lax.all_to_all(
        lax.all_to_all(
            along_kz.reshape(1, 1, length_z, block_x * block_y),
            "gx",
            split_axis=2,
            concat_axis=0,
            tiled=True,
        ),
        "gy",
        split_axis=2,
        concat_axis=1,
        tiled=True,
    )
    planes = planes.reshape(count_x, count_y, layers, block_x, block_y)
    split_x = table_x.reshape(full_x, count_x, block_x)
    split_y = table_y.reshape(full_y, count_y, block_y)
    partial_x = jnp.einsum("abkxy,iax->bkiy", planes, split_x, precision=highest)
    spectrum = jnp.einsum("bkiy,jby->kij", partial_x, split_y, precision=highest)
    modes_z = (
        lax.axis_index("gx") * (length_z // count_x)
        + lax.axis_index("gy") * layers
        + jnp.arange(layers)
    ).astype(jnp.float32)
    modes_x = jnp.arange(full_x, dtype=jnp.float32)
    modes_y = jnp.arange(full_y, dtype=jnp.float32)
    eigen_sum = (
        eigen_row(modes_z, length_z)[:, None, None]
        + eigen_row(modes_x, full_x)[None, :, None]
        + eigen_row(modes_y, full_y)[None, None, :]
    )
    zero_mode = (
        (modes_z == 0)[:, None, None]
        & (modes_x == 0)[None, :, None]
        & (modes_y == 0)[None, None, :]
    ).astype(jnp.float32)
    pressure_hat = -spectrum * (1.0 - zero_mode) / (eigen_sum + zero_mode)
    partial_back = jnp.einsum("kij,iax->kaxj", pressure_hat, split_x, precision=highest)
    blocks = jnp.einsum("kaxj,jby->abkxy", partial_back, split_y, precision=highest)
    next_x = jnp.concatenate(
        [blocks[1:, :, :, 0, :], jnp.zeros_like(blocks[:1, :, :, 0, :])], axis=0
    )
    next_y = jnp.concatenate(
        [blocks[:, 1:, :, :, 0], jnp.zeros_like(blocks[:, :1, :, :, 0])], axis=1
    )
    order_z = (
        table_z.reshape(count_x, count_y, layers, length_z)
        .transpose(1, 0, 2, 3)
        .reshape(length_z, length_z)
    )
    flat_shape = (count_x, count_y, layers, block_x * block_y)
    moved_p, moved_rx, moved_ry = (
        lax.all_to_all(
            lax.all_to_all(
                blocks.reshape(flat_shape), "gx", split_axis=0, concat_axis=2, tiled=True
            ),
            "gy",
            split_axis=1,
            concat_axis=2,
            tiled=True,
        ),
        lax.all_to_all(
            lax.all_to_all(next_x, "gx", split_axis=0, concat_axis=2, tiled=True),
            "gy",
            split_axis=1,
            concat_axis=2,
            tiled=True,
        ),
        lax.all_to_all(
            lax.all_to_all(next_y, "gx", split_axis=0, concat_axis=2, tiled=True),
            "gy",
            split_axis=1,
            concat_axis=2,
            tiled=True,
        ),
    )
    pressure = jnp.einsum(
        "kxy,kn->xyn", moved_p.reshape(length_z, block_x, block_y), order_z, precision=highest
    )
    rim_x = jnp.einsum("ky,kn->yn", moved_rx.reshape(length_z, block_y), order_z, precision=highest)
    rim_y = jnp.einsum("kx,kn->xn", moved_ry.reshape(length_z, block_x), order_z, precision=highest)
    grad_x = jnp.concatenate([pressure[1:], rim_x[None]], axis=0) - pressure
    grad_y = jnp.concatenate([pressure[:, 1:], rim_y[:, None]], axis=1) - pressure
    grad_z = jnp.concatenate(
        [pressure[:, :, 1:] - pressure[:, :, :-1], jnp.zeros_like(pressure[:, :, :1])], axis=2
    )
    projected = confine(
        jnp.stack([interior[0] - grad_x, interior[1] - grad_y, interior[2] - grad_z, interior[3]]),
        0,
    )[:3]
    return (projected, emission)


def solution(mesh):
    in_specs = (P(None, "gx", "gy", None), P("gx", "gy", None))
    out_specs = (P(None, "gx", "gy", None), P("gx", "gy", None))
    return jax.shard_map(
        per_device, mesh=mesh, in_specs=in_specs, out_specs=out_specs, check_vma=False
    )
```

profile of v0, /device:TPU:0, one launch (start us, length us, event | category | flops | bytes accessed | tf_op | source)
XLA Modules:
  0.0 226.9 jit_solution(3528422492842988513)
XLA Ops:
  0.6 1.3 convert_element_type.78
  1.9 1.0 bitcast_convert_fusion
  2.9 0.7 fusion.89
  3.7 4.8 %collective-permute-start = (f32[4,2,32,256]{3,2,1,0:T(8,128)}, f32[4,2,32,256]{3,2,1,0:T(8,128)S(1)}, u32[]{:S(2)}, u32[]{:S(2)}) collective-permute-start(f32[4,2,32,256]{3,2,1,0:T(8,128)} %get-tuple-element.59), channel_id=1, source_target_pairs={{0,8},{8,16},{16,24},{1,9},{9,17},{17,25},{2,10},{10,18},{18,26},{... | collective-permute-start | bytes 786440 | tf_op jit(solution)/shard_map/ppermute | solution.py:17
  8.5 1.3 collective-permute-start.1
  9.8 1.6 multiply_bitcast_fusion.11
  11.5 2.9 %collective-permute-done = f32[4,2,32,256]{3,2,1,0:T(8,128)S(1)} collective-permute-done((f32[4,2,32,256]{3,2,1,0:T(8,128)}, f32[4,2,32,256]{3,2,1,0:T(8,128)S(1)}, u32[]{:S(2)}, u32[]{:S(2)}) %collective-permute-start) | collective-permute-done | bytes 262176 | tf_op jit(solution)/shard_map/ppermute | solution.py:17
  14.4 7.5 %collective-permute-done.1 = f32[4,2,32,256]{3,2,1,0:T(8,128)S(1)} collective-permute-done((f32[4,2,32,256]{3,2,1,0:T(8,128)S(1)}, f32[4,2,32,256]{3,2,1,0:T(8,128)S(1)}, u32[]{:S(2)}, u32[]{:S(2)}) %collective-permute-start.1) | collective-permute-done | bytes 262176 | tf_op jit(solution)/shard_map/ppermute | solution.py:20
  22.0 1.3 collective-permute-start.2
  23.3 1.3 collective-permute-start.3
  25.2 3.2 %collective-permute-done.3 = f32[4,20,2,256]{3,2,1,0:T(2,128)S(1)} collective-permute-done((f32[4,20,2,256]{3,2,1,0:T(2,128)S(1)}, f32[4,20,2,256]{3,2,1,0:T(2,128)S(1)}, u32[]{:S(2)}, u32[]{:S(2)}) %collective-permute-start.3) | collective-permute-done | bytes 163872 | tf_op jit(solution)/shard_map/ppermute | solution.py:20
  28.4 3.3 %maximum_maximum_fusion.1 = (f32[4,20,34,256]{3,2,1,0:T(8,128)}, f32[4,20,34,256]{3,2,1,0:T(8,128)}) fusion(f32[4,2,32,256]{3,2,1,0:T(8,128)S(1)} %collective-permute-done.1, f32[1,16,32,256]{3,2,1,0:T(8,128)S(1)} %bitcast_convert_fusion, f32[3,16,32,256]{3,2,1,0:T(8,128)S(1)} %convert_element_type.78, f32[4,2,32,256]{3,2,1,0:T(8,128)S(1)} %collective-permute-done, ...), kind=kLoop, calls=%fused_computation.17 | loop fusion | flops 5570560 | bytes 8519680 | tf_op jit(solution)/shard_map/concatenate | solution.py:21
  32.9 8.9 %fusion.37 = f32[4,16,32,256]{3,2,1,0:T(8,128)} fusion(f32[4,20,36,256]{3,2,1,0:T(8,128)S(1)} %pad_maximum_fusion.3, f32[4,20,34,256]{3,2,1,0:T(8,128)} %get-tuple-element.48, f32[1,16,32,256]{3,2,1,0:T(8,128)S(1)} %bitcast_convert_fusion, f32[3,16,32,256]{3,2,1,0:T(8,128)S(1)} %convert_element_type.78, f32[4,20,34,256]{3,2,1,0:T(8,128)} %get-tuple-element.47, ...), kind=kLoop, calls=%fused_computation.65 | loop fusion | flops 25690112 | bytes 27066368 | tf_op jit(solution)/shard_map/add | solution.py:124
  41.7 1.8 slice_multiply_fusion.5
  43.6 0.8 pad_maximum_fusion.10
  44.4 3.4 %collective-permute-start.4 = (f32[4,3,32,256]{3,2,1,0:T(8,128)}, f32[4,3,32,256]{3,2,1,0:T(8,128)S(1)}, u32[]{:S(2)}, u32[]{:S(2)}) collective-permute-start(f32[4,3,32,256]{3,2,1,0:T(8,128)} %get-tuple-element.51), channel_id=1, source_target_pairs={{0,8},{8,16},{16,24},{1,9},{9,17},{17,25},{2,10},{10,18},{18,26},{... | collective-permute-start | bytes 1179656 | tf_op jit(solution)/shard_map/ppermute | solution.py:17
  47.8 1.3 collective-permute-start.5
  49.2 5.5 %collective-permute-done.4 = f32[4,3,32,256]{3,2,1,0:T(8,128)S(1)} collective-permute-done((f32[4,3,32,256]{3,2,1,0:T(8,128)}, f32[4,3,32,256]{3,2,1,0:T(8,128)S(1)}, u32[]{:S(2)}, u32[]{:S(2)}) %collective-permute-start.4) | collective-permute-done | bytes 393248 | tf_op jit(solution)/shard_map/ppermute | solution.py:17
  54.7 8.5 %collective-permute-done.5 = f32[4,3,32,256]{3,2,1,0:T(8,128)S(1)} collective-permute-done((f32[4,3,32,256]{3,2,1,0:T(8,128)S(1)}, f32[4,3,32,256]{3,2,1,0:T(8,128)S(1)}, u32[]{:S(2)}, u32[]{:S(2)}) %collective-permute-start.5) | collective-permute-done | bytes 393248 | tf_op jit(solution)/shard_map/ppermute | solution.py:20
  63.2 1.0 pad_maximum_fusion.16
  64.1 5.0 %collective-permute-start.6 = (f32[4,22,3,256]{3,2,1,0:T(4,128)}, f32[4,22,3,256]{3,2,1,0:T(4,128)S(1)}, u32[]{:S(2)}, u32[]{:S(2)}) collective-permute-start(f32[4,22,3,256]{3,2,1,0:T(4,128)} %get-tuple-element.45), channel_id=1, source_target_pairs={{0,1},{1,2},{2,3},{3,4},{4,5},{5,6},{6,7},{8,9},{9,10},{10,11},{11... | collective-permute-start | bytes 811016 | tf_op jit(solution)/shard_map/ppermute | solution.py:17
  69.1 1.5 collective-permute-start.7
  70.7 4.5 %collective-permute-done.7 = f32[4,22,3,256]{3,2,1,0:T(4,128)} collective-permute-done((f32[4,22,3,256]{3,2,1,0:T(4,128)}, f32[4,22,3,256]{3,2,1,0:T(4,128)}, u32[]{:S(2)}, u32[]{:S(2)}) %collective-permute-start.7) | collective-permute-done | bytes 270368 | tf_op jit(solution)/shard_map/ppermute | solution.py:20
  75.2 1.7 pad_maximum_fusion
  76.9 2.3 %multiply_bitcast_fusion.5 = (f32[18,34,256]{2,1,0:T(8,128)}, f32[18,34,256]{2,1,0:T(8,128)}, f32[18,34,256]{2,1,0:T(8,128)}, f32[18,34,256]{2,1,0:T(8,128)}, f32[18,34,256]{2,1,0:T(8,128)}, /*index=5*/f32[18,34,256]{2,1,0:T(8,128)}) fusion(f32[4,22,38,256]{3,2,1,0:T(8,128)S(1)} %pad_maximum_fusion), kind=kLoop, calls=%fused_computation.121 | loop fusion | flops 1880064 | bytes 5640192 | tf_op jit(solution)/shard_map/mul | solution.py:71
  79.3 2.2 maximum_maximum_fusion
  81.5 10.1 %fusion.8 = f32[4,18,34,256]{3,2,1,0:T(8,128)S(1)} fusion(f32[4,22,38,256]{3,2,1,0:T(8,128)S(1)} %pad_maximum_fusion, f32[4,22,35,256]{3,2,1,0:T(8,128)S(1)} %get-tuple-element.44, f32[4,22,35,256]{3,2,1,0:T(8,128)S(1)} %get-tuple-element.43, f32[4,20,36,256]{3,2,1,0:T(8,128)S(1)} %copy-done.1, f32[18,34,256]{2,1,0:T(8,128)} %get-tuple-element.37, ...), kind=kLoop, calls=%fused_computation.26 | loop fusion | flops 31334400 | bytes 39362560 | tf_op jit(solution)/shard_map/add | solution.py:128
  92.4 1.1 fusion.151
  93.5 0.9 copy-done.5
  94.4 1.7 fusion.75
  96.1 1.0 copy.26
  97.2 3.5 %all-to-all-start = ((f32[1,1,256,512]{3,1,0,2:T(1,128)}), f32[1,1,256,512]{3,1,0,2:T(1,128)S(1)}, u32[]{:S(2)}, u32[]{:S(2)}) async-start(f32[1,1,256,512]{3,1,0,2:T(1,128)} %copy.26), calls=%async_computation | async-start | bytes 1048576 | tf_op jit(solution)/shard_map/all_to_all | solution.py:167
  100.8 6.4 %all-to-all-done = f32[1,1,256,512]{3,1,0,2:T(1,128)S(1)} async-done(((f32[1,1,256,512]{3,1,0,2:T(1,128)}), f32[1,1,256,512]{3,1,0,2:T(1,128)S(1)}, u32[]{:S(2)}, u32[]{:S(2)}) %all-to-all-start) | async-done | bytes 524320 | tf_op jit(solution)/shard_map/all_to_all | solution.py:167
  107.2 1.1 copy.27
  108.4 10.3 %all-to-all-start.1 = ((f32[4,1,64,512]{3,0,1,2:T(4,128)}), f32[4,1,64,512]{3,0,1,2:T(4,128)S(1)}, u32[]{:S(2)}, u32[]{:S(2)}) async-start(f32[4,1,64,512]{3,0,1,2:T(4,128)} %copy.27), calls=%async_computation.1 | async-start | bytes 1048576 | tf_op jit(solution)/shard_map/all_to_all | solution.py:166
  118.9 15.1 %all-to-all-done.1 = f32[4,1,64,512]{3,0,1,2:T(4,128)S(1)} async-done(((f32[4,1,64,512]{3,0,1,2:T(4,128)}), f32[4,1,64,512]{3,0,1,2:T(4,128)S(1)}, u32[]{:S(2)}, u32[]{:S(2)}) %all-to-all-start.1) | async-done | bytes 524320 | tf_op jit(solution)/shard_map/all_to_all | solution.py:166
  134.7 3.4 %convolution_bitcast_fusion.1 = f32[8,8,64,32]{2,3,1,0:T(8,128)S(1)} fusion(f32[4,8,8,16,32]{4,3,0,2,1:T(8,128)S(1)} %reshape.642, f32[4,16]{1,0:T(4,128)S(1)} %add_add_fusion.1, f32[64]{0:T(128)S(1)} %get-tuple-element.87, f32[64]{0:T(128)S(1)} %get-tuple-element.88), kind=kOutput, calls=%fused_computation.98 | convolution fusion | flops 100675584 | bytes 1049344 | tf_op jit(solution)/shard_map/abkxy,iax->bkiy/dot_general | solution.py:182
  138.1 2.7 %fusion.65 = f32[8,64,256,1]{2,1,3,0:T(8,128)S(1)} fusion(f32[8,8,64,32]{2,3,1,0:T(8,128)S(1)} %convolution_bitcast_fusion.1, f32[256]{0:T(256)S(1)} %multiply_subtract_fusion.2, f32[8,64]{1,0:T(8,128)S(1)} %broadcast_add_fusion, pred[256]{0:T(512)(128)(4,1)S(1)} %iota_compare_fusion, pred[8,64]{1,0:T(8,128)(4,1)S(1)} %broadcast_and_fusion.2, ...), kind=kOutput, calls=%fused_computation.104 | convolution fusion | flops 403898368 | bytes 1055488 | tf_op jit(solution)/shard_map/bkiy,jby->kij/dot_general | solution.py:183
  140.8 0.7 convolution_bitcast_fusion.2
  141.6 2.7 %convolution_bitcast_fusion = f32[4,8,8,16,32]{4,3,0,2,1:T(8,128)S(1)} fusion(f32[8,4,16,256,1]{3,2,1,0,4:T(8,128)S(1)} %convolution_bitcast_fusion.2, f32[8,32]{1,0:T(8,128)S(1)} %add_add_fusion, f32[256]{0:T(256)S(1)} %get-tuple-element.86, f32[256]{0:T(256)S(1)} %broadcast_select_fusion), kind=kOutput, calls=%fused_computation.96 | convolution fusion | flops 402849792 | bytes 1051648 | tf_op jit(solution)/shard_map/kaxj,jby->abkxy/dot_general | solution.py:203
  144.3 1.4 slice.357
  145.7 2.9 %copy.37 = f32[4,7,8,16,1]{3,2,1,0,4:T(8,128)S(1)} copy(f32[4,7,8,16,1]{4,3,0,2,1:T(8,128)} %slice.357) | data formatting | bytes 28672 | tf_op jit(solution)/shard_map/slice | solution.py:208
  149.3 3.2 %all-to-all-start.6 = ((f32[4,1,1024]{2,1,0:T(1,128)}), f32[4,1,1024]{2,1,0:T(1,128)S(1)}, u32[]{:S(2)}, u32[]{:S(2)}) async-start(f32[4,1,1024]{2,1,0:T(1,128)} %reshape.643), calls=%async_computation.6 | async-start | bytes 32768 | tf_op jit(solution)/shard_map/all_to_all | solution.py:234
  152.6 0.7 reshape.647
  153.3 3.8 %all-to-all-done.6 = f32[4,1,1024]{2,1,0:T(1,128)S(1)} async-done(((f32[4,1,1024]{2,1,0:T(1,128)}), f32[4,1,1024]{2,1,0:T(1,128)S(1)}, u32[]{:S(2)}, u32[]{:S(2)}) %all-to-all-start.6) | async-done | bytes 16416 | tf_op jit(solution)/shard_map/all_to_all | solution.py:234
  157.2 3.3 %all-to-all-start.4 = ((f32[4,1,2048]{2,1,0:T(1,128)}), f32[4,1,2048]{2,1,0:T(1,128)S(1)}, u32[]{:S(2)}, u32[]{:S(2)}) async-start(f32[4,1,2048]{2,1,0:T(1,128)} %reshape.647), calls=%async_computation.4 | async-start | bytes 65536 | tf_op jit(solution)/shard_map/all_to_all | solution.py:227
  162.6 2.6 %all-to-all-done.4 = f32[4,1,2048]{2,1,0:T(1,128)S(1)} async-done(((f32[4,1,2048]{2,1,0:T(1,128)}), f32[4,1,2048]{2,1,0:T(1,128)S(1)}, u32[]{:S(2)}, u32[]{:S(2)}) %all-to-all-start.4) | async-done | bytes 32800 | tf_op jit(solution)/shard_map/all_to_all | solution.py:227
  165.2 3.5 %all-to-all-start.7 = ((f32[8,1,512]{2,1,0:T(1,128)}), f32[8,1,512]{2,1,0:T(1,128)S(1)}, u32[]{:S(2)}, u32[]{:S(2)}) async-start(f32[8,1,512]{2,1,0:T(1,128)} %reshape.645), calls=%async_computation.7 | async-start | bytes 32768 | tf_op jit(solution)/shard_map/all_to_all | solution.py:233
  168.7 0.8 reshape.624
  169.6 1.0 copy.30
  170.5 3.5 %all-to-all-done.7 = f32[8,1,512]{2,1,0:T(1,128)S(1)} async-done(((f32[8,1,512]{2,1,0:T(1,128)}), f32[8,1,512]{2,1,0:T(1,128)S(1)}, u32[]{:S(2)}, u32[]{:S(2)}) %all-to-all-start.7) | async-done | bytes 16416 | tf_op jit(solution)/shard_map/all_to_all | solution.py:233
  174.1 3.5 %all-to-all-start.2 = ((f32[4,8,8,512]{3,2,1,0:T(8,128)}), f32[4,8,8,512]{3,2,1,0:T(8,128)S(1)}, u32[]{:S(2)}, u32[]{:S(2)}) async-start(f32[4,8,8,512]{3,2,1,0:T(8,128)} %copy.30), calls=%async_computation.2 | async-start | bytes 1048576 | tf_op jit(solution)/shard_map/all_to_all | solution.py:218
  177.8 0.7 reduce
  179.4 6.3 %all-to-all-done.2 = f32[4,8,8,512]{3,2,1,0:T(8,128)S(1)} async-done(((f32[4,8,8,512]{3,2,1,0:T(8,128)}), f32[4,8,8,512]{3,2,1,0:T(8,128)S(1)}, u32[]{:S(2)}, u32[]{:S(2)}) %all-to-all-start.2) | async-done | bytes 524320 | tf_op jit(solution)/shard_map/all_to_all | solution.py:218
  185.7 3.3 %all-to-all-start.5 = ((f32[8,1,1024]{2,1,0:T(1,128)}), f32[8,1,1024]{2,1,0:T(1,128)S(1)}, u32[]{:S(2)}, u32[]{:S(2)}) async-start(f32[8,1,1024]{2,1,0:T(1,128)} %reshape.649), calls=%async_computation.5 | async-start | bytes 65536 | tf_op jit(solution)/shard_map/all_to_all | solution.py:226
  189.2 8.4 %all_gather.3 = f32[4,32,256]{2,1,0:T(8,128)S(1)} all-gather(f32[1,32,256]{2,1,0:T(8,128)S(1)} %slice.362), channel_id=1, replica_groups=mesh['gx'=4,'gy'=8] {'gx'}, dimensions={0}, use_global_device_ids=true | all-gather | bytes 163840 | tf_op jit(solution)/shard_map/all_gather | solution.py:27
  197.7 0.8 copy.56
  198.5 5.0 %all-to-all-start.3 = ((f32[1,8,32,512]{3,2,0,1:T(8,128)}), f32[1,8,32,512]{3,2,0,1:T(8,128)S(1)}, u32[]{:S(2)}, u32[]{:S(2)}) async-start(f32[1,8,32,512]{3,2,0,1:T(8,128)} %bitcast.195), calls=%async_computation.3 | async-start | bytes 1048576 | tf_op jit(solution)/shard_map/all_to_all | solution.py:217
  203.6 1.2 multiply_multiply_fusion
  205.6 1.2 fusion.96
  207.7 1.2 convolution_bitcast_fusion.4
  208.9 10.0 %all-to-all-done.3 = f32[1,8,32,512]{3,2,0,1:T(8,128)S(1)} async-done(((f32[1,8,32,512]{3,2,0,1:T(8,128)}), f32[1,8,32,512]{3,2,0,1:T(8,128)S(1)}, u32[]{:S(2)}, u32[]{:S(2)}) %all-to-all-start.3) | async-done | bytes 524320 | tf_op jit(solution)/shard_map/all_to_all | solution.py:217
  219.4 4.5 %fusion.60 = f32[16,32,256]{2,1,0:T(8,128)S(1)} fusion(f32[256,16,32]{2,1,0:T(8,128)S(1)} %reshape.625, f32[256]{0:T(256)S(1)} %mul.722, f32[256]{0:T(256)S(1)} %reshape.631, f32[256]{0:T(256)S(1)} %get-tuple-element.85), kind=kOutput, calls=%fused_computation.94 | convolution fusion | flops 402849792 | bytes 1051648 | tf_op jit(solution)/shard_map/kxy,kn->xyn/dot_general | solution.py:241
  225.6 1.2 pad_maximum_fusion.6
  (85 shorter events, 11.9 us)
Async XLA Ops:
  3.7 10.7 %collective-permute-start = (f32[4,2,32,256]{3,2,1,0:T(8,128)}, f32[4,2,32,256]{3,2,1,0:T(8,128)S(1)}, u32[]{:S(2)}, u32[]{:S(2)}) collective-permute-start(f32[4,2,32,256]{3,2,1,0:T(8,128)} %get-tuple-element.59), channel_id=1, source_target_pairs={{0,8},{8,16},{16,24},{1,9},{9,17},{17,25},{2,10},{10,18},{18,26},{... | collective-permute-start | bytes 786440 | tf_op jit(solution)/shard_map/ppermute | solution.py:17
  8.5 13.3 %collective-permute-start.1 = (f32[4,2,32,256]{3,2,1,0:T(8,128)S(1)}, f32[4,2,32,256]{3,2,1,0:T(8,128)S(1)}, u32[]{:S(2)}, u32[]{:S(2)}) collective-permute-start(f32[4,2,32,256]{3,2,1,0:T(8,128)S(1)} %get-tuple-element.60), channel_id=1, source_target_pairs={{8,0},{16,8},{24,16},{9,1},{17,9},{25,17},{10,2},{18,10},{26,18},{... | collective-permute-start | bytes 786440 | tf_op jit(solution)/shard_map/ppermute | solution.py:20
  22.0 3.2 %collective-permute-start.2 = (f32[4,20,2,256]{3,2,1,0:T(2,128)S(1)}, f32[4,20,2,256]{3,2,1,0:T(2,128)S(1)}, u32[]{:S(2)}, u32[]{:S(2)}) collective-permute-start(f32[4,20,2,256]{3,2,1,0:T(2,128)S(1)} %get-tuple-element.49), channel_id=1, source_target_pairs={{0,1},{1,2},{2,3},{3,4},{4,5},{5,6},{6,7},{8,9},{9,10},{10,11},{11... | collective-permute-start | bytes 491528 | tf_op jit(solution)/shard_map/ppermute | solution.py:17
  23.3 5.1 %collective-permute-start.3 = (f32[4,20,2,256]{3,2,1,0:T(2,128)S(1)}, f32[4,20,2,256]{3,2,1,0:T(2,128)S(1)}, u32[]{:S(2)}, u32[]{:S(2)}) collective-permute-start(f32[4,20,2,256]{3,2,1,0:T(2,128)S(1)} %get-tuple-element.50), channel_id=1, source_target_pairs={{1,0},{2,1},{3,2},{4,3},{5,4},{6,5},{7,6},{9,8},{10,9},{11,10},{12... | collective-permute-start | bytes 491528 | tf_op jit(solution)/shard_map/ppermute | solution.py:20
  31.7 1.0 copy-start.7
  31.7 1.2 copy-start.8
  32.3 9.5 %copy-start = (f32[4,20,36,256]{3,2,1,0:T(8,128)}, f32[4,20,36,256]{3,2,1,0:T(8,128)S(1)}, u32[]{:S(2)}) copy-start(f32[4,20,36,256]{3,2,1,0:T(8,128)S(1)} %pad_maximum_fusion.3) | copy-start | bytes 8847364
  44.4 10.3 %collective-permute-start.4 = (f32[4,3,32,256]{3,2,1,0:T(8,128)}, f32[4,3,32,256]{3,2,1,0:T(8,128)S(1)}, u32[]{:S(2)}, u32[]{:S(2)}) collective-permute-start(f32[4,3,32,256]{3,2,1,0:T(8,128)} %get-tuple-element.51), channel_id=1, source_target_pairs={{0,8},{8,16},{16,24},{1,9},{9,17},{17,25},{2,10},{10,18},{18,26},{... | collective-permute-start | bytes 1179656 | tf_op jit(solution)/shard_map/ppermute | solution.py:17
  47.8 15.3 %collective-permute-start.5 = (f32[4,3,32,256]{3,2,1,0:T(8,128)S(1)}, f32[4,3,32,256]{3,2,1,0:T(8,128)S(1)}, u32[]{:S(2)}, u32[]{:S(2)}) collective-permute-start(f32[4,3,32,256]{3,2,1,0:T(8,128)S(1)} %get-tuple-element.52), channel_id=1, source_target_pairs={{8,0},{16,8},{24,16},{9,1},{17,9},{25,17},{10,2},{18,10},{26,18},{... | collective-permute-start | bytes 1179656 | tf_op jit(solution)/shard_map/ppermute | solution.py:20
  64.1 6.6 %collective-permute-start.6 = (f32[4,22,3,256]{3,2,1,0:T(4,128)}, f32[4,22,3,256]{3,2,1,0:T(4,128)S(1)}, u32[]{:S(2)}, u32[]{:S(2)}) collective-permute-start(f32[4,22,3,256]{3,2,1,0:T(4,128)} %get-tuple-element.45), channel_id=1, source_target_pairs={{0,1},{1,2},{2,3},{3,4},{4,5},{5,6},{6,7},{8,9},{9,10},{10,11},{11... | collective-permute-start | bytes 811016 | tf_op jit(solution)/shard_map/ppermute | solution.py:17
  69.1 6.1 %collective-permute-start.7 = (f32[4,22,3,256]{3,2,1,0:T(4,128)}, f32[4,22,3,256]{3,2,1,0:T(4,128)}, u32[]{:S(2)}, u32[]{:S(2)}) collective-permute-start(f32[4,22,3,256]{3,2,1,0:T(4,128)} %get-tuple-element.46), channel_id=1, source_target_pairs={{1,0},{2,1},{3,2},{4,3},{5,4},{6,5},{7,6},{9,8},{10,9},{11,10},{12... | collective-permute-start | bytes 811016 | tf_op jit(solution)/shard_map/ppermute | solution.py:20
  79.3 2.2 copy-start.1
  93.5 0.9 copy-start.5
  93.5 14.8 %copy-start.3 = (f32[1,18,34,256]{3,2,1,0:T(8,128)}, f32[1,18,34,256]{3,2,1,0:T(8,128)S(1)}, u32[]{:S(2)}) copy-start(f32[1,18,34,256]{3,2,1,0:T(8,128)S(1)} %get-tuple-element.41) | copy-start | bytes 1880068
  97.2 10.0 %all-to-all-start = ((f32[1,1,256,512]{3,1,0,2:T(1,128)}), f32[1,1,256,512]{3,1,0,2:T(1,128)S(1)}, u32[]{:S(2)}, u32[]{:S(2)}) async-start(f32[1,1,256,512]{3,1,0,2:T(1,128)} %copy.26), calls=%async_computation | async-start | bytes 1048576 | tf_op jit(solution)/shard_map/all_to_all | solution.py:167
  108.4 25.7 %all-to-all-start.1 = ((f32[4,1,64,512]{3,0,1,2:T(4,128)}), f32[4,1,64,512]{3,0,1,2:T(4,128)S(1)}, u32[]{:S(2)}, u32[]{:S(2)}) async-start(f32[4,1,64,512]{3,0,1,2:T(4,128)} %copy.27), calls=%async_computation.1 | async-start | bytes 1048576 | tf_op jit(solution)/shard_map/all_to_all | solution.py:166
  149.3 7.9 %all-to-all-start.6 = ((f32[4,1,1024]{2,1,0:T(1,128)}), f32[4,1,1024]{2,1,0:T(1,128)S(1)}, u32[]{:S(2)}, u32[]{:S(2)}) async-start(f32[4,1,1024]{2,1,0:T(1,128)} %reshape.643), calls=%async_computation.6 | async-start | bytes 32768 | tf_op jit(solution)/shard_map/all_to_all | solution.py:234
  157.2 8.0 %all-to-all-start.4 = ((f32[4,1,2048]{2,1,0:T(1,128)}), f32[4,1,2048]{2,1,0:T(1,128)S(1)}, u32[]{:S(2)}, u32[]{:S(2)}) async-start(f32[4,1,2048]{2,1,0:T(1,128)} %reshape.647), calls=%async_computation.4 | async-start | bytes 65536 | tf_op jit(solution)/shard_map/all_to_all | solution.py:227
  165.2 8.9 %all-to-all-start.7 = ((f32[8,1,512]{2,1,0:T(1,128)}), f32[8,1,512]{2,1,0:T(1,128)S(1)}, u32[]{:S(2)}, u32[]{:S(2)}) async-start(f32[8,1,512]{2,1,0:T(1,128)} %reshape.645), calls=%async_computation.7 | async-start | bytes 32768 | tf_op jit(solution)/shard_map/all_to_all | solution.py:233
  169.6 19.5 %copy-start.2 = (f32[1,18,34,256]{3,2,1,0:T(8,128)S(1)}, f32[1,18,34,256]{3,2,1,0:T(8,128)}, u32[]{:S(2)}) copy-start(f32[1,18,34,256]{3,2,1,0:T(8,128)} %get-tuple-element.40) | copy-start | bytes 1880068
  174.1 11.7 %all-to-all-start.2 = ((f32[4,8,8,512]{3,2,1,0:T(8,128)}), f32[4,8,8,512]{3,2,1,0:T(8,128)S(1)}, u32[]{:S(2)}, u32[]{:S(2)}) async-start(f32[4,8,8,512]{3,2,1,0:T(8,128)} %copy.30), calls=%async_computation.2 | async-start | bytes 1048576 | tf_op jit(solution)/shard_map/all_to_all | solution.py:218
  185.7 12.8 %all-to-all-start.5 = ((f32[8,1,1024]{2,1,0:T(1,128)}), f32[8,1,1024]{2,1,0:T(1,128)S(1)}, u32[]{:S(2)}, u32[]{:S(2)}) async-start(f32[8,1,1024]{2,1,0:T(1,128)} %reshape.649), calls=%async_computation.5 | async-start | bytes 65536 | tf_op jit(solution)/shard_map/all_to_all | solution.py:226
  198.5 20.4 %all-to-all-start.3 = ((f32[1,8,32,512]{3,2,0,1:T(8,128)}), f32[1,8,32,512]{3,2,0,1:T(8,128)S(1)}, u32[]{:S(2)}, u32[]{:S(2)}) async-start(f32[1,8,32,512]{3,2,0,1:T(8,128)} %bitcast.195), calls=%async_computation.3 | async-start | bytes 1048576 | tf_op jit(solution)/shard_map/all_to_all | solution.py:217
  224.0 1.1 copy-start.4
  224.0 1.3 copy-start.6
where the time goes:
time: 228 us; the launch traced here: 227 us
  waiting for transfers between devices  79.8 us (35%)
  starting transfers between devices  55.5 us (24%)
  other arithmetic  46.3 us (20%)
  matrix products  18.3 us (8%)
  local copies, waits for them, and re-layouts  17.4 us (8%)
  blocking collectives  8.44 us (4%)
    ppermute x4, waiting for transfers between devices, padded_2(): lax.ppermute(lax.slice_in_dim(block, 0, width, axis=dim), axis, backward)  23.6 us
    all_to_all x1, waiting for transfers between devices, per_device(): lax.all_to_all(lax.all_to_all(along_kz.reshape(1, 1, length_z, block_x *...  15.1 us
    ppermute x4, starting transfers between devices, padded_2(): lax.ppermute(lax.slice_in_dim(block, block.shape[dim] - width, None, axis...  14.5 us
    all_to_all x1, starting transfers between devices, per_device(): lax.all_to_all(lax.all_to_all(along_kz.reshape(1, 1, length_z, block_x *...  10.3 us
    add x1, other arithmetic, per_device(): 0.5 * earlier  10.1 us
    all_to_all x1, waiting for transfers between devices, per_device(): lax.all_to_all(lax.all_to_all(blocks.reshape(flat_shape), 'gx', split_axi...  9.98 us
    add x1, other arithmetic, per_device(): section_one = confine(fields + time_step * tendency_rim(widened), 0)  8.85 us
    all_gather x1, blocking collectives, entering(): gathered = lax.all_gather(part, axis)  8.44 us
  transfers between devices with their start and end apart: 16, of which 13 were waited for; matrix products, arithmetic and copies ran while one was open for 7% of the time, Pallas kernels for 0%

commit v1 on v0

v1 whole, which is shorter than its diff:
```python
import functools

import jax
import jax.numpy as jnp
from jax import lax
from jax.experimental import pallas as pl
from jax.experimental.pallas import tpu as pltpu
from jax.sharding import PartitionSpec as P
import numpy as np

time_step = 0.4
buoyancy = 2.0
extinction = 3.0
highest = lax.Precision.HIGHEST


def padded_2(block, sides, width):
    for axis, dim in sides:
        count = lax.axis_size(axis)
        forward = [(i, i + 1) for i in range(count - 1)]
        backward = [(target, source) for source, target in forward]
        low = lax.ppermute(
            lax.slice_in_dim(block, block.shape[dim] - width, None, axis=dim), axis, forward
        )
        high = lax.ppermute(lax.slice_in_dim(block, 0, width, axis=dim), axis, backward)
        block = jnp.concatenate([low, block, high], axis=dim)
    return block


def cosine_table(length):
    modes = np.arange(length)[:, None]
    centres = np.arange(length)[None, :] + 0.5
    factor = np.where(modes == 0, np.sqrt(1.0 / length), np.sqrt(2.0 / length))
    return (factor * np.cos(np.pi * modes * centres / length)).astype(np.float32)


def flux_terms(padded):
    extent = padded.shape

    def window(offset_x, offset_y, offset_z):
        return padded[
            :,
            2 + offset_x : extent[1] - 2 + offset_x,
            2 + offset_y : extent[2] - 2 + offset_y,
            2 + offset_z : extent[3] - 2 + offset_z,
        ]

    def moved(axis_id, offset):
        offsets = [0, 0, 0]
        offsets[axis_id] = offset
        return window(offsets[0], offsets[1], offsets[2])

    middle = window(0, 0, 0)
    summed = jnp.zeros_like(middle)
    for axis_id in range(3):
        plus_one = moved(axis_id, 1)
        plus_two = moved(axis_id, 2)
        minus_one = moved(axis_id, -1)
        minus_two = moved(axis_id, -2)
        lower_diff = (2.0 * plus_one + 3.0 * middle - 6.0 * minus_one + minus_two) / 6.0
        upper_diff = (-plus_two + 6.0 * plus_one - 3.0 * middle - 2.0 * minus_one) / 6.0
        speed_axis = middle[axis_id]
        summed = (
            summed
            + jnp.maximum(speed_axis, 0.0) * lower_diff
            + jnp.minimum(speed_axis, 0.0) * upper_diff
        )
    return -summed


def tendency_rim(extended):
    return flux_terms(jnp.pad(extended, ((0, 0), (0, 0), (0, 0), (2, 2))))


def cropped(extended, have_rim, want_rim):
    cut_size = have_rim - want_rim
    return extended[
        :, cut_size : extended.shape[1] - cut_size, cut_size : extended.shape[2] - cut_size, :
    ]


def advect_halo(fields, rim_width):
    return padded_2(fields, (("gx", 1), ("gy", 2)), rim_width)


def halves(value):
    big = value.astype(jnp.bfloat16)
    return big, (value - big.astype(jnp.float32)).astype(jnp.bfloat16)


def dot_split(left, right):
    left_big, left_rest = halves(left)
    right_big, right_rest = halves(right)

    def dot(one, two):
        return jnp.dot(one, two, preferred_element_type=jnp.float32)

    return dot(left_big, right_big) + (dot(left_big, right_rest) + dot(left_rest, right_big))


def mode_tables(full_x, length_z, slab, groups, anchor_kz):
    modes_x = jnp.arange(full_x, dtype=jnp.float32)[:, None]
    modes_z = (anchor_kz + jnp.arange(slab * groups) % slab).astype(jnp.float32)[None, :]
    shift = 4.0 * (
        jnp.sin(modes_x * (np.pi / (2 * full_x))) ** 2
        + jnp.sin(modes_z * (np.pi / (2 * length_z))) ** 2
    )
    root = jnp.sqrt(shift + 0.25 * shift * shift)
    decay = 1.0 / (1.0 + 0.5 * shift + root)
    zero = (modes_x == 0) & (modes_z == 0)
    gain = jnp.where(zero, 0.0, -0.5 / jnp.where(zero, 1.0, root))
    return decay, gain


def solve_kernel(
    count_x,
    count_y,
    div_ref,
    lifted_ref,
    total_ref,
    tz_ref,
    tzt_ref,
    tx_ref,
    txt_ref,
    decay_ref,
    gain_ref,
    out_ref,
    before_ref,
    send_a,
    recv_a,
    send_b,
    recv_b,
    send_e,
    recv_e,
    edge,
    totals,
    sums,
    hat,
    sems_x,
    sems_y,
):
    block_x, block_y, length_z = div_ref.shape
    full_x = block_x * count_x
    me_x = lax.axis_index("gx")
    me_y = lax.axis_index("gy")
    slab = length_z // count_x
    lanes = recv_a.shape[-1]
    groups = lanes // slab
    rows = block_y // groups

    barrier = pltpu.get_barrier_semaphore()
    for offset in range(1, count_x):
        pl.semaphore_signal(
            barrier,
            inc=1,
            device_id={"gx": lax.rem(me_x + offset, count_x)},
            device_id_type=pl.DeviceIdType.MESH,
        )
    for offset in range(1, count_y):
        pl.semaphore_signal(
            barrier,
            inc=1,
            device_id={"gy": lax.rem(me_y + offset, count_y)},
            device_id_type=pl.DeviceIdType.MESH,
        )
    div = jnp.swapaxes(div_ref[...], 0, 1).reshape(block_y * block_x, length_z)
    along = dot_split(div, tzt_ref[...]).reshape(block_y, block_x, length_z)
    for target in range(count_x):
        send_a[target] = jnp.concatenate(
            [
                along[group * rows : (group + 1) * rows, :, target * slab : (target + 1) * slab]
                for group in range(groups)
            ],
            axis=-1,
        )
    pl.semaphore_wait(barrier, count_x + count_y - 2)

    def to_x(kind, source, target):
        copies = []
        for offset in range(1, count_x):
            to = lax.rem(me_x + offset, count_x)
            copies.append(
                pltpu.make_async_remote_copy(
                    src_ref=source.at[to] if source is not total_ref else source,
                    dst_ref=target.at[me_x],
                    send_sem=sems_x.at[kind, 0, offset],
                    recv_sem=sems_x.at[kind, 1, offset],
                    device_id={"gx": to},
                    device_id_type=pl.DeviceIdType.MESH,
                )
            )
        for copy in copies:
            copy.start()
        return copies

    copies_a = to_x(0, send_a, recv_a)
    copies_t = to_x(1, total_ref, totals)
    recv_a[me_x] = send_a[me_x]

    lane = lax.broadcasted_iota(jnp.int32, (full_x, lanes), 1)
    group_of = lane // slab
    decay = decay_ref[...]
    gain = gain_ref[...]
    zero = gain == 0.0

    def power(base, count):
        result = None
        while count:
            if count & 1:
                result = base if result is None else result * base
            count >>= 1
            if count:
                base = base * base
        return result

    def up(value):
        return pltpu.roll(value, slab, 1)

    def down(value):
        return pltpu.roll(value, lanes - slab, 1)

    decay_rows = power(decay, rows)
    decay_block = power(decay_rows, groups)
    decay_full = power(decay_block, count_y)

    for copy in copies_a:
        copy.wait()
    gathered = jnp.concatenate(
        [
            jnp.concatenate([recv_a[place, row] for place in range(count_x)], axis=0)
            for row in range(rows)
        ],
        axis=1,
    )
    modes = dot_split(tx_ref[...], gathered)
    for row in range(rows):
        hat[row] = modes[:, row * lanes : (row + 1) * lanes]

    forward = hat[0]
    for row in range(1, rows):
        forward = decay * forward + hat[row]
    backward = hat[rows - 1]
    for row in range(rows - 2, -1, -1):
        backward = decay * backward + hat[row]
    forward_block = forward
    for group in range(1, groups):
        forward_block = jnp.where(
            group_of == group, forward + decay_rows * up(forward_block), forward_block
        )
    backward_block = backward
    for group in range(groups - 2, -1, -1):
        backward_block = jnp.where(
            group_of == group, backward + decay_rows * down(backward_block), backward_block
        )
    sums[me_y] = jnp.where(group_of == 0, backward_block, forward_block)
    copies_s = []
    for offset in range(1, count_y):
        copies_s.append(
            pltpu.make_async_remote_copy(
                src_ref=sums.at[me_y],
                dst_ref=sums.at[me_y],
                send_sem=sems_y.at[0, offset],
                recv_sem=sems_y.at[1, offset],
                device_id={"gy": lax.rem(me_y + offset, count_y)},
                device_id_type=pl.DeviceIdType.MESH,
            )
        )
    for copy in copies_s:
        copy.start()
    for copy in copies_s:
        copy.wait()

    from_low = jnp.zeros_like(decay)
    all_low = jnp.zeros_like(decay)
    power_low = jnp.ones_like(decay)
    from_high = jnp.zeros_like(decay)
    all_high = jnp.zeros_like(decay)
    power_high = jnp.ones_like(decay)
    for place in range(count_y):
        part = sums[place]
        all_low = all_low * decay_block + part
        from_low = jnp.where(place < me_y, from_low * decay_block + part, from_low)
        power_low = jnp.where(place < me_y, power_low * decay_block, power_low)
        other = count_y - 1 - place
        part = sums[other]
        all_high = all_high * decay_block + part
        from_high = jnp.where(other > me_y, from_high * decay_block + part, from_high)
        power_high = jnp.where(other > me_y, power_high * decay_block, power_high)
    first = group_of == 0

    def swap(value):
        return up(value) if groups == 2 else jnp.where(first, up(value), down(value))

    whole = jnp.where(first, all_high, all_low)
    image = jnp.where(
        zero,
        0.0,
        (whole + decay_full * swap(whole)) / jnp.where(zero, 1.0, 1.0 - decay_full * decay_full),
    )
    entering = jnp.where(first, from_high, from_low) + jnp.where(
        first, power_high, power_low
    ) * swap(image)
    carry_up = up(entering)
    for group in range(1, groups):
        carry_up = jnp.where(group_of == group, up(forward + decay_rows * carry_up), carry_up)
    carry_down = down(entering)
    for group in range(groups - 2, -1, -1):
        carry_down = jnp.where(
            group_of == group, down(backward + decay_rows * carry_down), carry_down
        )

    top = slice(0, 8)
    mean = jnp.where(first, whole, up(whole))
    for group in range(2, groups):
        mean = jnp.where(group_of == group, up(mean), mean)
    mean = mean[top] * (1.0 / (block_y * count_y))
    flat = jnp.zeros_like(mean)
    flats = [flat]
    position = (me_y * block_y + group_of[top] * rows).astype(jnp.float32)
    ahead = carry_up
    left = [ahead]
    for row in range(rows):
        ahead = decay * ahead + hat[row]
        left.append(ahead)
        flat = flat + (ahead[top] - (position + (row + 1.0)) * mean)
        flats.append(flat)
    offset_flat = jnp.zeros_like(mean)
    for group in range(1, groups):
        offset_flat = jnp.where(
            group_of[top] == group, up(offset_flat + flats[rows]), offset_flat
        )
    behind = carry_down
    pressures = [None] * (rows + 1)
    for row in range(rows, -1, -1):
        if row < rows:
            behind = decay * behind + hat[row]
        pressure = gain * (decay * left[row] + behind)
        special = jnp.where(zero[top], flats[row] + offset_flat, pressure[top])
        pressures[row] = jnp.concatenate([special, pressure[8:]], axis=0)
    back = dot_split(txt_ref[...], jnp.concatenate(pressures, axis=1))
    for target in range(count_x):
        for row in range(rows + 1):
            columns = slice(row * lanes, (row + 1) * lanes)
            send_b[target, row] = back[target * block_x : (target + 1) * block_x, columns]
            if target < count_x - 1:
                after = (target + 1) * block_x
                send_e[target, row : row + 1, :] = back[after : after + 1, columns]
        if target == count_x - 1:
            send_e[target] = jnp.zeros(send_e.shape[1:], jnp.float32)
    copies_b = to_x(2, send_b, recv_b)
    copies_e = to_x(3, send_e, recv_e)
    recv_b[me_x] = send_b[me_x]
    recv_e[me_x] = send_e[me_x]
    for copy in copies_t:
        copy.wait()
    before = jnp.zeros_like(before_ref)
    for place in range(count_x - 1):
        before = jnp.where(place < me_x, before + totals[place], before)
    before_ref[...] = before
    for copy in copies_b + copies_e:
        copy.wait()

    def spread(ref):
        parts = []
        for group in range(groups):
            size = rows + (group == groups - 1)
            parts.append(
                jnp.concatenate(
                    [
                        ref[place][:size, ..., group * slab : (group + 1) * slab]
                        for place in range(count_x)
                    ],
                    axis=-1,
                )
            )
        return parts

    table = tz_ref[...]
    field = jnp.concatenate(spread(recv_b), axis=0)
    field = dot_split(field.reshape((block_y + 1) * block_x, length_z), table)
    field = field.reshape(block_y + 1, block_x, length_z)
    for group, part in enumerate(spread(recv_e)):
        edge[group * rows : group * rows + part.shape[0], :] = part
    following = dot_split(edge[...], table)[:block_y]
    middle = field[:block_y]
    last_x = lax.broadcasted_iota(jnp.int32, middle.shape, 1) == block_x - 1
    ahead_x = jnp.where(last_x, following[:, None, :], jnp.roll(middle, -1, axis=1))
    ahead_z = pltpu.roll(middle, length_z - 1, 2)
    gradients = (ahead_x - middle, field[1:] - middle, ahead_z - middle)
    place_x = lax.broadcasted_iota(jnp.int32, div_ref.shape, 0) + me_x * block_x
    place_y = lax.broadcasted_iota(jnp.int32, div_ref.shape, 1) + me_y * block_y
    place_z = lax.broadcasted_iota(jnp.int32, div_ref.shape, 2)
    opened = (
        place_x < full_x - 1,
        place_y < block_y * count_y - 1,
        place_z < length_z - 1,
    )
    for axis_id in range(3):
        value = lifted_ref[axis_id] - jnp.swapaxes(gradients[axis_id], 0, 1)
        out_ref[axis_id] = jnp.where(opened[axis_id], value, 0.0)


def pressure_solve(divergence, lifted, total):
    block_x, block_y, length_z = divergence.shape
    count_x = lax.axis_size("gx")
    count_y = lax.axis_size("gy")
    full_x = block_x * count_x
    slab = length_z // count_x
    lanes = 128
    groups = lanes // slab
    rows = block_y // groups
    padded = -(-(rows + 1) // 8) * 8
    table_z = cosine_table(length_z)
    table_x = cosine_table(full_x)
    decay, gain = mode_tables(full_x, length_z, slab, groups, lax.axis_index("gx") * slab)
    vmem = pl.BlockSpec(memory_space=pltpu.VMEM)

    def buffer(*shape):
        return pltpu.VMEM(shape, jnp.float32)

    return pl.pallas_call(
        functools.partial(solve_kernel, count_x, count_y),
        out_shape=(
            jax.ShapeDtypeStruct(lifted.shape, jnp.float32),
            jax.ShapeDtypeStruct(total.shape, jnp.float32),
        ),
        in_specs=[vmem] * 9,
        out_specs=(vmem, vmem),
        scratch_shapes=[
            buffer(count_x, rows, block_x, lanes),
            buffer(count_x, rows, block_x, lanes),
            buffer(count_x, rows + 1, block_x, lanes),
            buffer(count_x, rows + 1, block_x, lanes),
            buffer(count_x, padded, lanes),
            buffer(count_x, padded, lanes),
            buffer(block_y + 8, length_z),
            buffer(count_x, *total.shape),
            buffer(count_y, full_x, lanes),
            buffer(rows, full_x, lanes),
            pltpu.SemaphoreType.DMA((4, 2, count_x)),
            pltpu.SemaphoreType.DMA((2, count_y)),
        ],
        compiler_params=pltpu.CompilerParams(
            collective_id=0, has_side_effects=True, vmem_limit_bytes=48 * 1024 * 1024
        ),
    )(
        divergence,
        lifted,
        total,
        jnp.asarray(table_z),
        jnp.asarray(table_z.T.copy()),
        jnp.asarray(table_x),
        jnp.asarray(table_x.T.copy()),
        decay,
        gain,
    )


def per_device(velocity, density):
    block_x, block_y, length_z = density.shape
    count_x = lax.axis_size("gx")
    count_y = lax.axis_size("gy")
    full_x = block_x * count_x
    full_y = block_y * count_y
    anchor_x = lax.axis_index("gx") * block_x
    anchor_y = lax.axis_index("gy") * block_y

    def confine(fields, rim_width):
        along_x = anchor_x - rim_width + jnp.arange(block_x + 2 * rim_width)
        along_y = anchor_y - rim_width + jnp.arange(block_y + 2 * rim_width)
        along_z = jnp.arange(length_z)
        inside = ((along_x >= 0) & (along_x < full_x))[:, None, None] & (
            (along_y >= 0) & (along_y < full_y)
        )[None, :, None]
        open_x = inside & (along_x < full_x - 1)[:, None, None]
        open_y = inside & (along_y < full_y - 1)[None, :, None]
        open_z = inside & (along_z < length_z - 1)[None, None, :]
        return jnp.stack(
            [fields[0] * open_x, fields[1] * open_y, fields[2] * open_z, fields[3] * inside]
        )

    fields = jnp.concatenate(
        [velocity.astype(jnp.float32), density.astype(jnp.float32)[None]], axis=0
    )
    widened = advect_halo(fields, 2)
    section_one = confine(fields + time_step * tendency_rim(widened), 0)
    section_one = advect_halo(section_one, 3)
    earlier = cropped(widened, 2, 1)
    section_two = confine(
        0.5 * earlier + 0.5 * (cropped(section_one, 3, 1) + time_step * tendency_rim(section_one)),
        1,
    )
    smoke_now = section_two[3]
    smoke_above = jnp.concatenate(
        [smoke_now[:, :, 1:], jnp.zeros_like(smoke_now[:, :, :1])], axis=2
    )
    lifted = confine(
        jnp.stack(
            [
                section_two[0],
                section_two[1],
                section_two[2] + time_step * buoyancy * 0.5 * (smoke_now + smoke_above),
                smoke_now,
            ]
        ),
        1,
    )
    interior = lifted[:, 1:-1, 1:-1, :]
    below_z = jnp.concatenate(
        [jnp.zeros_like(interior[2][:, :, :1]), interior[2][:, :, :-1]], axis=2
    )
    divergence = (
        interior[0]
        - lifted[0, :-2, 1:-1, :]
        + (interior[1] - lifted[1, 1:-1, :-2, :])
        + (interior[2] - below_z)
    )
    column = interior[3]
    attenuation = extinction / full_x
    running = jnp.cumsum(column, axis=0)
    projected, before = pressure_solve(divergence, interior[:3], running[-1])
    optical = attenuation * (before[None] + running - column)
    emission = jnp.exp(-optical) * -jnp.expm1(-attenuation * column) / attenuation
    return (projected, emission)


def solution(mesh):
    in_specs = (P(None, "gx", "gy", None), P("gx", "gy", None))
    out_specs = (P(None, "gx", "gy", None), P("gx", "gy", None))
    return jax.shard_map(
        per_device, mesh=mesh, in_specs=in_specs, out_specs=out_specs, check_vma=False
    )
```

time: 228 us -> 127 us (0.56)
  waiting for transfers between devices: 79.8 us -> 31.4 us
  starting transfers between devices: 55.5 us -> 19.9 us
  Pallas kernels: 0 us -> 33.2 us
  matrix products: 18.3 us -> 0 us
  local copies, waits for them, and re-layouts: 17.4 us -> 3.5 us
  other arithmetic: 46.3 us -> 37.8 us
  blocking collectives: 8.44 us -> 0 us
    all_to_all x8 -> x0, waiting for transfers between devices: 47.8 us -> none  [the longest x1 15.1 us: per_device(): lax.all_to_all(lax.all_to_all(along_kz.reshape(1, 1, length_z, block_x *...]
    all_to_all x8 -> x0, starting transfers between devices: 35.6 us -> none  [the longest x1 10.3 us: per_device(): lax.all_to_all(lax.all_to_all(along_kz.reshape(1, 1, length_z, block_x *...]
    pallas_call x0 -> x1, Pallas kernels: none -> 33.2 us  [pressure_solve(): pl.pallas_call(functools.partial(solve_kernel, count_x, count_y), out_sha...]
    dot_general x8 -> x0, matrix products: 18.3 us -> none  [the longest x1 4.53 us: per_device(): jnp.einsum('kxy,kn->xyn', moved_p.reshape(length_z, block_x, block_y), or...]
    all_gather x1 -> x0, blocking collectives: 8.44 us -> none  [entering(): gathered = lax.all_gather(part, axis)]
    slice x7 -> x0, local copies, waits for them, and re-layouts: 4.4 us -> none  [the longest x2 4.23 us: per_device(): blocks[:, 1:, :, :, 0]]
    reshape x6 -> x0, local copies, waits for them, and re-layouts: 4.08 us -> none  [the longest x2 1.79 us: per_device(): blocks.reshape(flat_shape)]
    all_to_all x4 -> x0, other arithmetic: 2.78 us -> none  [the longest x1 0.72 us: per_device(): lax.all_to_all(next_x, 'gx', split_axis=0, concat_axis=2, tiled=True)]
  transfers between devices with their start and end apart: 16 -> 8, of which waited for: 13 -> 6; matrix products, arithmetic and copies ran while one was open for 7% -> 2% of each run, Pallas kernels for 0% -> 0%
where the time goes in v1:
time: 127 us
  other arithmetic  37.8 us (30%)
  Pallas kernels  33.2 us (26%)
  waiting for transfers between devices  31.4 us (25%)
  starting transfers between devices  19.9 us (16%)
  local copies, waits for them, and re-layouts  3.5 us (3%)
    pallas_call x1, Pallas kernels, pressure_solve(): pl.pallas_call(functools.partial(solve_kernel, count_x, count_y), out_sha...  33.2 us
    ppermute x4, waiting for transfers between devices, padded_2(): lax.ppermute(lax.slice_in_dim(block, 0, width, axis=dim), axis, backward)  23.2 us
    ppermute x4, starting transfers between devices, padded_2(): lax.ppermute(lax.slice_in_dim(block, block.shape[dim] - width, None, axis...  14.5 us
    add x1, other arithmetic, per_device(): 0.5 * earlier  9.98 us
    add x1, other arithmetic, per_device(): section_one = confine(fields + time_step * tendency_rim(widened), 0)  8.86 us
    ppermute x4, waiting for transfers between devices, padded_2(): lax.ppermute(lax.slice_in_dim(block, block.shape[dim] - width, None, axis...  8.21 us
    concatenate x5, other arithmetic, padded_2(): block = jnp.concatenate([low, block, high], axis=dim)  6.41 us
    ppermute x4, starting transfers between devices, padded_2(): lax.ppermute(lax.slice_in_dim(block, 0, width, axis=dim), axis, backward)  5.35 us
  transfers between devices with their start and end apart: 8, of which 6 were waited for; matrix products, arithmetic and copies ran while one was open for 2% of the time, Pallas kernels for 0%

profile of v1, /device:TPU:0, one launch (start us, length us, event | category | flops | bytes accessed | tf_op | source)
XLA Modules:
  0.0 126.7 jit_solution(4550375198312498347)
XLA Ops:
  0.6 1.3 %convert_element_type.72 = f32[3,16,32,256]{3,2,1,0:T(8,128)S(1)} convert(bf16[3,16,32,256]{3,2,1,0:T(8,128)(2,1)} %param.6) | non-fusion elementwise | flops 393216 | bytes 2359296 | tf_op jit(solution)/shard_map/convert_element_type | solution.py:483
  1.9 1.0 bitcast_convert_fusion
  2.9 0.7 fusion.71
  3.7 4.8 %collective-permute-start = (f32[4,2,32,256]{3,2,1,0:T(8,128)}, f32[4,2,32,256]{3,2,1,0:T(8,128)S(1)}, u32[]{:S(2)}, u32[]{:S(2)}) collective-permute-start(f32[4,2,32,256]{3,2,1,0:T(8,128)} %get-tuple-element.31), channel_id=1, source_target_pairs={{0,8},{8,16},{16,24},{1,9},{9,17},{17,25},{2,10},{10,18},{18,26},{... | collective-permute-start | bytes 786440 | tf_op jit(solution)/shard_map/ppermute | solution.py:22
  8.5 1.3 %collective-permute-start.1 = (f32[4,2,32,256]{3,2,1,0:T(8,128)S(1)}, f32[4,2,32,256]{3,2,1,0:T(8,128)S(1)}, u32[]{:S(2)}, u32[]{:S(2)}) collective-permute-start(f32[4,2,32,256]{3,2,1,0:T(8,128)S(1)} %get-tuple-element.32), channel_id=1, source_target_pairs={{8,0},{16,8},{24,16},{9,1},{17,9},{25,17},{10,2},{18,10},{26,18},{... | collective-permute-start | bytes 786440 | tf_op jit(solution)/shard_map/ppermute | solution.py:25
  9.8 1.6 %multiply_bitcast_fusion.11 = (f32[16,32,256]{2,1,0:T(8,128)S(1)}, f32[16,32,256]{2,1,0:T(8,128)}, f32[16,32,256]{2,1,0:T(8,128)}, f32[16,32,256]{2,1,0:T(8,128)...) fusion(f32[3,16,32,256]{3,2,1,0:T(8,128)S(1)} %convert_element_type.72), kind=kLoop, calls=%fused_computation.130 | loop fusion | flops 1572864 | bytes 4718592 | tf_op jit(solution)/shard_map/mul | solution.py:65
  11.5 0.1 and_convert_fusion.4
  11.6 2.8 %collective-permute-done = f32[4,2,32,256]{3,2,1,0:T(8,128)S(1)} collective-permute-done((f32[4,2,32,256]{3,2,1,0:T(8,128)}, f32[4,2,32,256]{3,2,1,0:T(8,128)S(1)}, u32[]{:S(2)}, u32[]{:S(2)}) %collective-permute-start) | collective-permute-done | bytes 262176 | tf_op jit(solution)/shard_map/ppermute | solution.py:22
  14.4 7.5 %collective-permute-done.1 = f32[4,2,32,256]{3,2,1,0:T(8,128)S(1)} collective-permute-done((f32[4,2,32,256]{3,2,1,0:T(8,128)S(1)}, f32[4,2,32,256]{3,2,1,0:T(8,128)S(1)}, u32[]{:S(2)}, u32[]{:S(2)}) %collective-permute-start.1) | collective-permute-done | bytes 262176 | tf_op jit(solution)/shard_map/ppermute | solution.py:25
  21.9 0.1 pad_maximum_fusion.21
  22.0 1.3 %collective-permute-start.2 = (f32[4,20,2,256]{3,2,1,0:T(2,128)S(1)}, f32[4,20,2,256]{3,2,1,0:T(2,128)S(1)}, u32[]{:S(2)}, u32[]{:S(2)}) collective-permute-start(f32[4,20,2,256]{3,2,1,0:T(2,128)S(1)} %get-tuple-element.21), channel_id=1, source_target_pairs={{0,1},{1,2},{2,3},{3,4},{4,5},{5,6},{6,7},{8,9},{9,10},{10,11},{11... | collective-permute-start | bytes 491528 | tf_op jit(solution)/shard_map/ppermute | solution.py:22
  23.3 1.3 %collective-permute-start.3 = (f32[4,20,2,256]{3,2,1,0:T(2,128)S(1)}, f32[4,20,2,256]{3,2,1,0:T(2,128)S(1)}, u32[]{:S(2)}, u32[]{:S(2)}) collective-permute-start(f32[4,20,2,256]{3,2,1,0:T(2,128)S(1)} %get-tuple-element.22), channel_id=1, source_target_pairs={{1,0},{2,1},{3,2},{4,3},{5,4},{6,5},{7,6},{9,8},{10,9},{11,10},{12... | collective-permute-start | bytes 491528 | tf_op jit(solution)/shard_map/ppermute | solution.py:25
  24.6 0.6 maximum_maximum_fusion.2
  25.2 0.0 collective-permute-done.2
  25.2 3.2 %collective-permute-done.3 = f32[4,20,2,256]{3,2,1,0:T(2,128)S(1)} collective-permute-done((f32[4,20,2,256]{3,2,1,0:T(2,128)S(1)}, f32[4,20,2,256]{3,2,1,0:T(2,128)S(1)}, u32[]{:S(2)}, u32[]{:S(2)}) %collective-permute-start.3) | collective-permute-done | bytes 163872 | tf_op jit(solution)/shard_map/ppermute | solution.py:25
  28.4 3.4 %maximum_maximum_fusion.1 = (f32[4,20,34,256]{3,2,1,0:T(8,128)}, f32[4,20,34,256]{3,2,1,0:T(8,128)}) fusion(f32[4,2,32,256]{3,2,1,0:T(8,128)S(1)} %collective-permute-done.1, f32[1,16,32,256]{3,2,1,0:T(8,128)S(1)} %bitcast_convert_fusion, f32[3,16,32,256]{3,2,1,0:T(8,128)S(1)} %convert_element_type.72, f32[4,2,32,256]{3,2,1,0:T(8,128)S(1)} %collective-permute-done, ...), kind=kLoop, calls=%fused_computation.16 | loop fusion | flops 5570560 | bytes 8519680 | tf_op jit(solution)/shard_map/concatenate | solution.py:26
  31.7 0.0 copy-start.6
  31.7 0.0 copy-start.7
  31.7 0.6 pad_maximum_fusion.3
  32.3 0.0 copy-start.4
  32.3 0.5 copy-done.6
  32.8 0.2 copy-done.7
  32.9 8.9 %fusion.37 = f32[4,16,32,256]{3,2,1,0:T(8,128)} fusion(f32[4,20,36,256]{3,2,1,0:T(8,128)S(1)} %pad_maximum_fusion.3, f32[4,20,34,256]{3,2,1,0:T(8,128)} %get-tuple-element.20, f32[1,16,32,256]{3,2,1,0:T(8,128)S(1)} %bitcast_convert_fusion, f32[3,16,32,256]{3,2,1,0:T(8,128)S(1)} %convert_element_type.72, f32[4,20,34,256]{3,2,1,0:T(8,128)} %get-tuple-element.19, ...), kind=kLoop, calls=%fused_computation.64 | loop fusion | flops 25690112 | bytes 27066368 | tf_op jit(solution)/shard_map/add | solution.py:486
  41.8 0.0 copy-done.4
  41.8 1.9 %slice_multiply_fusion.5 = (f32[1,16,32,256]{3,2,1,0:T(8,128)S(1)}, f32[1,16,32,256]{3,2,1,0:T(8,128)S(1)}, f32[1,16,32,256]{3,2,1,0:T(8,128)S(1)}, f32[1,16,32,256]{3,2,1,0:T(8,128)S(1)}) fusion(f32[4,16,32,256]{3,2,1,0:T(8,128)} %fusion.37, f32[16,32]{1,0:T(8,128)S(1)} %get-tuple-element.45, f32[16,32]{1,0:T(8,128)S(1)} %get-tuple-element.46, ...), kind=kLoop, calls=%fused_computation.123 | loop fusion | flops 655360 | bytes 4201216 | tf_op jit(solution)/shard_map/mul | solution.py:479
  43.7 0.8 pad_maximum_fusion.11
  44.5 3.4 %collective-permute-start.4 = (f32[4,3,32,256]{3,2,1,0:T(8,128)}, f32[4,3,32,256]{3,2,1,0:T(8,128)S(1)}, u32[]{:S(2)}, u32[]{:S(2)}) collective-permute-start(f32[4,3,32,256]{3,2,1,0:T(8,128)} %get-tuple-element.23), channel_id=1, source_target_pairs={{0,8},{8,16},{16,24},{1,9},{9,17},{17,25},{2,10},{10,18},{18,26},{... | collective-permute-start | bytes 1179656 | tf_op jit(solution)/shard_map/ppermute | solution.py:22
  47.9 1.3 %collective-permute-start.5 = (f32[4,3,32,256]{3,2,1,0:T(8,128)S(1)}, f32[4,3,32,256]{3,2,1,0:T(8,128)S(1)}, u32[]{:S(2)}, u32[]{:S(2)}) collective-permute-start(f32[4,3,32,256]{3,2,1,0:T(8,128)S(1)} %get-tuple-element.24), channel_id=1, source_target_pairs={{8,0},{16,8},{24,16},{9,1},{17,9},{25,17},{10,2},{18,10},{26,18},{... | collective-permute-start | bytes 1179656 | tf_op jit(solution)/shard_map/ppermute | solution.py:25
  49.2 0.1 broadcast_and_fusion
  49.3 5.4 %collective-permute-done.4 = f32[4,3,32,256]{3,2,1,0:T(8,128)S(1)} collective-permute-done((f32[4,3,32,256]{3,2,1,0:T(8,128)}, f32[4,3,32,256]{3,2,1,0:T(8,128)S(1)}, u32[]{:S(2)}, u32[]{:S(2)}) %collective-permute-start.4) | collective-permute-done | bytes 393248 | tf_op jit(solution)/shard_map/ppermute | solution.py:22
  54.7 8.5 %collective-permute-done.5 = f32[4,3,32,256]{3,2,1,0:T(8,128)S(1)} collective-permute-done((f32[4,3,32,256]{3,2,1,0:T(8,128)S(1)}, f32[4,3,32,256]{3,2,1,0:T(8,128)S(1)}, u32[]{:S(2)}, u32[]{:S(2)}) %collective-permute-start.5) | collective-permute-done | bytes 393248 | tf_op jit(solution)/shard_map/ppermute | solution.py:25
  63.2 0.1 pad_maximum_fusion.17
  63.4 5.0 %collective-permute-start.6 = (f32[4,22,3,256]{3,2,1,0:T(4,128)S(1)}, f32[4,22,3,256]{3,2,1,0:T(4,128)S(1)}, u32[]{:S(2)}, u32[]{:S(2)}) collective-permute-start(f32[4,22,3,256]{3,2,1,0:T(4,128)S(1)} %get-tuple-element.17), channel_id=1, source_target_pairs={{0,1},{1,2},{2,3},{3,4},{4,5},{5,6},{6,7},{8,9},{9,10},{10,11},{11... | collective-permute-start | bytes 811016 | tf_op jit(solution)/shard_map/ppermute | solution.py:22
  68.3 1.5 %collective-permute-start.7 = (f32[4,22,3,256]{3,2,1,0:T(4,128)S(1)}, f32[4,22,3,256]{3,2,1,0:T(4,128)S(1)}, u32[]{:S(2)}, u32[]{:S(2)}) collective-permute-start(f32[4,22,3,256]{3,2,1,0:T(4,128)S(1)} %get-tuple-element.18), channel_id=1, source_target_pairs={{1,0},{2,1},{3,2},{4,3},{5,4},{6,5},{7,6},{9,8},{10,9},{11,10},{12... | collective-permute-start | bytes 811016 | tf_op jit(solution)/shard_map/ppermute | solution.py:25
  69.9 0.1 slice.334
  69.9 0.1 and_select_fusion.2
  70.1 0.0 collective-permute-done.6
  70.1 4.0 %collective-permute-done.7 = f32[4,22,3,256]{3,2,1,0:T(4,128)S(1)} collective-permute-done((f32[4,22,3,256]{3,2,1,0:T(4,128)S(1)}, f32[4,22,3,256]{3,2,1,0:T(4,128)S(1)}, u32[]{:S(2)}, u32[]{:S(2)}) %collective-permute-start.7) | collective-permute-done | bytes 270368 | tf_op jit(solution)/shard_map/ppermute | solution.py:25
  74.1 0.8 pad_maximum_fusion
  74.9 2.0 %multiply_bitcast_fusion.5 = (f32[18,34,256]{2,1,0:T(8,128)S(1)}, f32[18,34,256]{2,1,0:T(8,128)S(1)}, f32[18,34,256]{2,1,0:T(8,128)}, f32[18,34,256]{2,1,0:T(8,1...) fusion(f32[4,22,38,256]{3,2,1,0:T(8,128)S(1)} %pad_maximum_fusion), kind=kLoop, calls=%fused_computation.110 | loop fusion | flops 1880064 | bytes 5640192 | tf_op jit(solution)/shard_map/mul | solution.py:65
  76.9 0.0 copy-start.5
  76.9 1.1 maximum_maximum_fusion
  78.0 0.8 copy-done.5
  78.8 10.0 %fusion.8 = f32[4,18,34,256]{3,2,1,0:T(8,128)S(1)} fusion(f32[4,22,38,256]{3,2,1,0:T(8,128)S(1)} %pad_maximum_fusion, f32[4,22,35,256]{3,2,1,0:T(8,128)S(1)} %get-tuple-element.16, f32[4,22,35,256]{3,2,1,0:T(8,128)S(1)} %get-tuple-element.15, f32[4,20,36,256]{3,2,1,0:T(8,128)S(1)} %copy-done.5, f32[18,34,256]{2,1,0:T(8,128)} %get-tuple-element.9, ...), kind=kLoop, calls=%fused_computation.25 | loop fusion | flops 31334400 | bytes 39583744 | tf_op jit(solution)/shard_map/add | solution.py:490
  88.8 0.2 bitcast_multiply_fusion
  88.9 0.3 slice.330
  89.2 0.3 fusion.61
  89.5 0.1 slice_bitcast_fusion.1
  89.6 0.3 fusion.86
  89.9 0.2 pad_maximum_fusion.6.lifted_ref
  90.1 0.0 copy-start
  90.1 0.0 copy-start.1
  90.1 0.0 copy-start.2
  90.1 0.0 copy-start.3
  90.1 0.3 fusion.68.div_ref
  90.4 0.1 fusion.69
  90.6 0.4 copy-done
  91.0 0.1 copy-done.1
  91.1 0.0 copy-done.2
  91.1 0.0 copy-done.3
  91.1 33.2 %shard_map.77 = (f32[3,16,32,256]{3,2,1,0:T(8,128)S(1)}, f32[32,256]{1,0:T(8,128)S(1)}) custom-call(f32[16,32,256]{2,1,0:T(8,128)S(1)} %fusion.68.div_ref, f32[3,16,32,256]{3,2,1,0:T(8,128)S(1)} %pad_maximum_fusion.6.lifted_ref, f32[32,256]{1,0:T(8,128)S(1)} %slice_bitcast_fusion.2.total_ref, f32[256,256]{1,0:T(8,128)S(1)} %copy-done, ...), custom_call_target="tpu_custom_call" | custom-call | tf_op jit(solution)/shard_map/pallas_call | solution.py:421
  124.3 1.2 multiply_multiply_fusion
  125.5 1.1 copy.9
  (10 shorter events, 0.2 us)
Async XLA Ops:
  3.7 10.7 %collective-permute-start = (f32[4,2,32,256]{3,2,1,0:T(8,128)}, f32[4,2,32,256]{3,2,1,0:T(8,128)S(1)}, u32[]{:S(2)}, u32[]{:S(2)}) collective-permute-start(f32[4,2,32,256]{3,2,1,0:T(8,128)} %get-tuple-element.31), channel_id=1, source_target_pairs={{0,8},{8,16},{16,24},{1,9},{9,17},{17,25},{2,10},{10,18},{18,26},{... | collective-permute-start | bytes 786440 | tf_op jit(solution)/shard_map/ppermute | solution.py:22
  8.5 13.3 %collective-permute-start.1 = (f32[4,2,32,256]{3,2,1,0:T(8,128)S(1)}, f32[4,2,32,256]{3,2,1,0:T(8,128)S(1)}, u32[]{:S(2)}, u32[]{:S(2)}) collective-permute-start(f32[4,2,32,256]{3,2,1,0:T(8,128)S(1)} %get-tuple-element.32), channel_id=1, source_target_pairs={{8,0},{16,8},{24,16},{9,1},{17,9},{25,17},{10,2},{18,10},{26,18},{... | collective-permute-start | bytes 786440 | tf_op jit(solution)/shard_map/ppermute | solution.py:25
  22.0 3.2 %collective-permute-start.2 = (f32[4,20,2,256]{3,2,1,0:T(2,128)S(1)}, f32[4,20,2,256]{3,2,1,0:T(2,128)S(1)}, u32[]{:S(2)}, u32[]{:S(2)}) collective-permute-start(f32[4,20,2,256]{3,2,1,0:T(2,128)S(1)} %get-tuple-element.21), channel_id=1, source_target_pairs={{0,1},{1,2},{2,3},{3,4},{4,5},{5,6},{6,7},{8,9},{9,10},{10,11},{11... | collective-permute-start | bytes 491528 | tf_op jit(solution)/shard_map/ppermute | solution.py:22
  23.3 5.1 %collective-permute-start.3 = (f32[4,20,2,256]{3,2,1,0:T(2,128)S(1)}, f32[4,20,2,256]{3,2,1,0:T(2,128)S(1)}, u32[]{:S(2)}, u32[]{:S(2)}) collective-permute-start(f32[4,20,2,256]{3,2,1,0:T(2,128)S(1)} %get-tuple-element.22), channel_id=1, source_target_pairs={{1,0},{2,1},{3,2},{4,3},{5,4},{6,5},{7,6},{9,8},{10,9},{11,10},{12... | collective-permute-start | bytes 491528 | tf_op jit(solution)/shard_map/ppermute | solution.py:25
  31.7 1.0 copy-start.6
  31.7 1.2 copy-start.7
  32.3 9.5 %copy-start.4 = (f32[4,20,36,256]{3,2,1,0:T(8,128)}, f32[4,20,36,256]{3,2,1,0:T(8,128)S(1)}, u32[]{:S(2)}) copy-start(f32[4,20,36,256]{3,2,1,0:T(8,128)S(1)} %pad_maximum_fusion.3) | copy-start | bytes 8847364
  44.5 10.3 %collective-permute-start.4 = (f32[4,3,32,256]{3,2,1,0:T(8,128)}, f32[4,3,32,256]{3,2,1,0:T(8,128)S(1)}, u32[]{:S(2)}, u32[]{:S(2)}) collective-permute-start(f32[4,3,32,256]{3,2,1,0:T(8,128)} %get-tuple-element.23), channel_id=1, source_target_pairs={{0,8},{8,16},{16,24},{1,9},{9,17},{17,25},{2,10},{10,18},{18,26},{... | collective-permute-start | bytes 1179656 | tf_op jit(solution)/shard_map/ppermute | solution.py:22
  47.9 15.3 %collective-permute-start.5 = (f32[4,3,32,256]{3,2,1,0:T(8,128)S(1)}, f32[4,3,32,256]{3,2,1,0:T(8,128)S(1)}, u32[]{:S(2)}, u32[]{:S(2)}) collective-permute-start(f32[4,3,32,256]{3,2,1,0:T(8,128)S(1)} %get-tuple-element.24), channel_id=1, source_target_pairs={{8,0},{16,8},{24,16},{9,1},{17,9},{25,17},{10,2},{18,10},{26,18},{... | collective-permute-start | bytes 1179656 | tf_op jit(solution)/shard_map/ppermute | solution.py:25
  63.4 6.7 %collective-permute-start.6 = (f32[4,22,3,256]{3,2,1,0:T(4,128)S(1)}, f32[4,22,3,256]{3,2,1,0:T(4,128)S(1)}, u32[]{:S(2)}, u32[]{:S(2)}) collective-permute-start(f32[4,22,3,256]{3,2,1,0:T(4,128)S(1)} %get-tuple-element.17), channel_id=1, source_target_pairs={{0,1},{1,2},{2,3},{3,4},{4,5},{5,6},{6,7},{8,9},{9,10},{10,11},{11... | collective-permute-start | bytes 811016 | tf_op jit(solution)/shard_map/ppermute | solution.py:22
  68.3 5.7 %collective-permute-start.7 = (f32[4,22,3,256]{3,2,1,0:T(4,128)S(1)}, f32[4,22,3,256]{3,2,1,0:T(4,128)S(1)}, u32[]{:S(2)}, u32[]{:S(2)}) collective-permute-start(f32[4,22,3,256]{3,2,1,0:T(4,128)S(1)} %get-tuple-element.18), channel_id=1, source_target_pairs={{1,0},{2,1},{3,2},{4,3},{5,4},{6,5},{7,6},{9,8},{10,9},{11,10},{12... | collective-permute-start | bytes 811016 | tf_op jit(solution)/shard_map/ppermute | solution.py:25
  76.9 1.9 %copy-start.5 = (f32[4,20,36,256]{3,2,1,0:T(8,128)S(1)}, f32[4,20,36,256]{3,2,1,0:T(8,128)}, u32[]{:S(2)}) copy-start(f32[4,20,36,256]{3,2,1,0:T(8,128)} %copy-done.4) | copy-start | bytes 8847364
  90.1 1.0 copy-start
  90.1 1.0 copy-start.1
  90.1 1.0 copy-start.2
  90.1 1.0 copy-start.3

commit v2 on v1

--- a/solution.py
+++ b/solution.py
@@ -14,19 +14,6 @@
 highest = lax.Precision.HIGHEST
 
 
-def padded_2(block, sides, width):
-    for axis, dim in sides:
-        count = lax.axis_size(axis)
-        forward = [(i, i + 1) for i in range(count - 1)]
-        backward = [(target, source) for source, target in forward]
-        low = lax.ppermute(
-            lax.slice_in_dim(block, block.shape[dim] - width, None, axis=dim), axis, forward
-        )
-        high = lax.ppermute(lax.slice_in_dim(block, 0, width, axis=dim), axis, backward)
-        block = jnp.concatenate([low, block, high], axis=dim)
-    return block
-
-
 def cosine_table(length):
     modes = np.arange(length)[:, None]
     centres = np.arange(length)[None, :] + 0.5
@@ -34,53 +21,263 @@
     return (factor * np.cos(np.pi * modes * centres / length)).astype(np.float32)
 
 
-def flux_terms(padded):
-    extent = padded.shape
-
-    def window(offset_x, offset_y, offset_z):
-        return padded[
-            :,
-            2 + offset_x : extent[1] - 2 + offset_x,
-            2 + offset_y : extent[2] - 2 + offset_y,
-            2 + offset_z : extent[3] - 2 + offset_z,
+def advect_kernel(
+    count_x,
+    count_y,
+    velocity_ref,
+    density_ref,
+    lifted_ref,
+    smoke_ref,
+    div_ref,
+    wide,
+    middle,
+    face_x,
+    face_y,
+    sent,
+    received,
+):
+    block_x, block_y, length_z = density_ref.shape
+    me_x = lax.axis_index("gx")
+    me_y = lax.axis_index("gy")
+    last_x = block_x * count_x - 1
+    last_y = block_y * count_y - 1
+    low_y, high_y, rim = 16, 16 + block_y, 8
+    moves = (
+        (1, 0, (0, 4), (block_x + 1, 1, 4), (low_y, low_y, block_y)),
+        (1, 0, (0, 1), (block_x, 0, 1), (low_y, low_y, block_y)),
+        (-1, 0, (0, 4), (5, block_x + 5, 4), (low_y, low_y, block_y)),
+        (1, 1, (0, 4), (block_x + 1, 1, 4), (high_y - rim, low_y - rim, rim)),
+        (1, -1, (0, 4), (block_x + 1, 1, 4), (low_y, high_y, rim)),
+        (-1, 1, (0, 4), (5, block_x + 5, 4), (high_y - rim, low_y - rim, rim)),
+        (-1, -1, (0, 4), (5, block_x + 5, 4), (low_y, high_y, rim)),
+        (0, 1, (0, 4), (5, 5, block_x), (high_y - rim, low_y - rim, rim)),
+        (0, -1, (0, 4), (5, 5, block_x), (low_y, high_y, rim)),
+    )
+
+    def exists(offset_x, offset_y):
+        to_x = me_x + offset_x
+        to_y = me_y + offset_y
+        return (to_x >= 0) & (to_x < count_x) & (to_y >= 0) & (to_y < count_y)
+
+    def copy_of(index):
+        offset_x, offset_y, fields, along_x, along_y = moves[index]
+        return pltpu.make_async_remote_copy(
+            src_ref=wide.at[
+                pl.ds(*fields), pl.ds(along_x[0], along_x[2]), pl.ds(along_y[0], along_y[2])
+            ],
+            dst_ref=wide.at[
+                pl.ds(*fields), pl.ds(along_x[1], along_x[2]), pl.ds(along_y[1], along_y[2])
+            ],
+            send_sem=sent.at[index],
+            recv_sem=received.at[index],
+            device_id={"gx": me_x + offset_x, "gy": me_y + offset_y},
+            device_id_type=pl.DeviceIdType.MESH,
+        )
+
+    around = [(i, j) for i in (-1, 0, 1) for j in (-1, 0, 1) if (i, j) != (0, 0)]
+    barrier = pltpu.get_barrier_semaphore()
+    for offset_x, offset_y in around:
+
+        @pl.when(exists(offset_x, offset_y))
+        def _():
+            pl.semaphore_signal(
+                barrier,
+                inc=1,
+                device_id={"gx": me_x + offset_x, "gy": me_y + offset_y},
+                device_id_type=pl.DeviceIdType.MESH,
+            )
+
+    for field in range(3):
+        wide[field, 5 : 5 + block_x, low_y:high_y, :] = velocity_ref[field].astype(jnp.float32)
+    wide[3, 5 : 5 + block_x, low_y:high_y, :] = density_ref[...].astype(jnp.float32)
+    span_x = 3 - (me_x == 0).astype(jnp.int32) - (me_x == count_x - 1).astype(jnp.int32)
+    span_y = 3 - (me_y == 0).astype(jnp.int32) - (me_y == count_y - 1).astype(jnp.int32)
+    pl.semaphore_wait(barrier, span_x * span_y - 1)
+
+    for index, move in enumerate(moves):
+
+        @pl.when(exists(move[0], move[1]))
+        def _():
+            copy_of(index).start()
+
+    for index, move in enumerate(moves):
+        fields, along_x, along_y = move[2:]
+
+        @pl.when(jnp.logical_not(exists(-move[0], -move[1])))
+        def _():
+            shape = (fields[1], along_x[2], along_y[2], length_z)
+            wide[
+                0 : fields[1],
+                along_x[1] : along_x[1] + along_x[2],
+                along_y[1] : along_y[1] + along_y[2],
+                :,
+            ] = jnp.zeros(shape, jnp.float32)
+
+    def arrive(indices):
+        for index in indices:
+
+            @pl.when(exists(-moves[index][0], -moves[index][1]))
+            def _():
+                copy_of(index).wait_recv()
+
+    lane = lax.broadcasted_iota(jnp.int32, (8, length_z), 1)
+    line = lax.broadcasted_iota(jnp.int32, (8, length_z), 0)
+    scale = -time_step / 12.0
+
+    def advance(source, at_x, at_y, fields):
+        centres = [source[field, at_x, at_y : at_y + 8, :] for field in range(4)]
+        weights = []
+        base = None
+        for axis_id in range(3):
+            speed = scale * centres[axis_id]
+            size = jnp.abs(speed)
+            eight = 8.0 * speed
+            four = 4.0 * size
+            parts = {1: four + eight, -1: four - eight, 2: -speed - size, -2: speed - size}
+            if axis_id == 2:
+                parts[1] = jnp.where(lane < length_z - 1, parts[1], 0.0)
+                parts[2] = jnp.where(lane < length_z - 2, parts[2], 0.0)
+                parts[-1] = jnp.where(lane > 0, parts[-1], 0.0)
+                parts[-2] = jnp.where(lane > 1, parts[-2], 0.0)
+            weights.append(parts)
+            base = size if base is None else base + size
+        base = 1.0 - 6.0 * base
+        results = []
+        for field in fields:
+            total = centres[field] * base
+            for offset in (-2, -1, 1, 2):
+                total = total + weights[0][offset] * source[
+                    field, at_x + offset, at_y : at_y + 8, :
+                ]
+                total = total + weights[1][offset] * source[
+                    field, at_x, at_y + offset : at_y + offset + 8, :
+                ]
+                total = total + weights[2][offset] * pltpu.roll(
+                    centres[field], (-offset) % length_z, 1
+                )
+            results.append(total)
+        return results
+
+    def walled(field, value, at_x, at_y):
+        if field == 0:
+            return value * jnp.where(me_x * block_x + at_x == last_x, 0.0, 1.0)
+        if field == 1:
+            return jnp.where(me_y * block_y + at_y + line == last_y, 0.0, value)
+        if field == 2:
+            return jnp.where(lane == length_z - 1, 0.0, value)
+        return value
+
+    def first_rows(start, stop, fields=(0, 1, 2, 3), tiles=None):
+        tiles = range(low_y - rim, high_y + rim, 8) if tiles is None else tiles
+
+        def row(at, carry):
+            for at_y in tiles:
+                values = advance(wide, at + 2, at_y, fields)
+                for field, value in zip(fields, values):
+                    middle[field, at, at_y : at_y + 8, :] = walled(
+                        field, value, at - 3, at_y - low_y
+                    )
+            return carry
+
+        lax.fori_loop(start + 3, stop + 3, row, 0)
+
+    def second(at_x, at_y, fields):
+        values = advance(middle, at_x + 3, at_y, fields)
+        return [
+            0.5 * wide[field, at_x + 5, at_y : at_y + 8, :] + 0.5 * value
+            for field, value in zip(fields, values)
         ]
 
-    def moved(axis_id, offset):
-        offsets = [0, 0, 0]
-        offsets[axis_id] = offset
-        return window(offsets[0], offsets[1], offsets[2])
-
-    middle = window(0, 0, 0)
-    summed = jnp.zeros_like(middle)
-    for axis_id in range(3):
-        plus_one = moved(axis_id, 1)
-        plus_two = moved(axis_id, 2)
-        minus_one = moved(axis_id, -1)
-        minus_two = moved(axis_id, -2)
-        lower_diff = (2.0 * plus_one + 3.0 * middle - 6.0 * minus_one + minus_two) / 6.0
-        upper_diff = (-plus_two + 6.0 * plus_one - 3.0 * middle - 2.0 * minus_one) / 6.0
-        speed_axis = middle[axis_id]
-        summed = (
-            summed
-            + jnp.maximum(speed_axis, 0.0) * lower_diff
-            + jnp.minimum(speed_axis, 0.0) * upper_diff
-        )
-    return -summed
-
-
-def tendency_rim(extended):
-    return flux_terms(jnp.pad(extended, ((0, 0), (0, 0), (0, 0), (2, 2))))
-
-
-def cropped(extended, have_rim, want_rim):
-    cut_size = have_rim - want_rim
-    return extended[
-        :, cut_size : extended.shape[1] - cut_size, cut_size : extended.shape[2] - cut_size, :
-    ]
-
-
-def advect_halo(fields, rim_width):
-    return padded_2(fields, (("gx", 1), ("gy", 2)), rim_width)
+    inside = range(low_y, high_y, 8)
+
+    def second_rows(start, stop):
+        def row(at_x, carry):
+            (value,) = second(at_x, low_y - 8, (1,))
+            face_y[at_x, 0:8, :] = walled(1, value, at_x, -8)
+            for at_y in inside:
+                near = at_y - low_y
+                part_x, part_y, part_z, smoke = second(at_x, at_y, (0, 1, 2, 3))
+                above = pltpu.roll(smoke, length_z - 1, 1)
+                part_z = part_z + (time_step * buoyancy * 0.5) * (smoke + above)
+                face_x[at_x + 1, near : near + 8, :] = walled(0, part_x, at_x, near)
+                face_y[at_x, near + 8 : near + 16, :] = walled(1, part_y, at_x, near)
+                lifted_ref[2, at_x, near : near + 8, :] = walled(2, part_z, at_x, near)
+                smoke_ref[at_x, near : near + 8, :] = smoke
+            return carry
+
+        lax.fori_loop(start, stop, row, 0)
+
+    arrive((7, 8))
+    first_rows(2, block_x - 2)
+    second_rows(4, block_x - 4)
+    arrive(range(7))
+    first_rows(-3, -2, (0,), inside)
+    first_rows(-2, 2)
+    first_rows(block_x - 2, block_x + 2)
+    for at_y in inside:
+        (value,) = second(-1, at_y, (0,))
+        face_x[0, at_y - low_y : at_y - low_y + 8, :] = walled(0, value, -1, 0)
+    second_rows(0, 4)
+    second_rows(block_x - 4, block_x)
+
+    def differ(at_x, carry):
+        part_x = face_x[at_x + 1]
+        part_y = face_y[at_x, 8 : 8 + block_y, :]
+        part_z = lifted_ref[2, at_x]
+        below = jnp.where(
+            lax.broadcasted_iota(jnp.int32, part_z.shape, 1) > 0, pltpu.roll(part_z, 1, 1), 0.0
+        )
+        lifted_ref[0, at_x] = part_x
+        lifted_ref[1, at_x] = part_y
+        div_ref[at_x] = (
+            part_x
+            - face_x[at_x]
+            + (part_y - face_y[at_x, 7 : 7 + block_y, :])
+            + (part_z - below)
+        )
+        return carry
+
+    lax.fori_loop(0, block_x, differ, 0)
+    for index, move in enumerate(moves):
+
+        @pl.when(exists(move[0], move[1]))
+        def _():
+            copy_of(index).wait_send()
+
+
+def advect(velocity, density):
+    block_x, block_y, length_z = density.shape
+    count_x = lax.axis_size("gx")
+    count_y = lax.axis_size("gy")
+    vmem = pl.BlockSpec(memory_space=pltpu.VMEM)
+
+    def buffer(*shape):
+        return pltpu.VMEM(shape, jnp.float32)
+
+    def result(*shape):
+        return jax.ShapeDtypeStruct(shape, jnp.float32)
+
+    return pl.pallas_call(
+        functools.partial(advect_kernel, count_x, count_y),
+        out_shape=(
+            result(3, *density.shape),
+            result(*density.shape),
+            result(*density.shape),
+        ),
+        in_specs=[vmem] * 2,
+        out_specs=(vmem,) * 3,
+        scratch_shapes=[
+            buffer(4, block_x + 9, block_y + 32, length_z),
+            buffer(4, block_x + 5, block_y + 32, length_z),
+            buffer(block_x + 1, block_y, length_z),
+            buffer(block_x, block_y + 8, length_z),
+            pltpu.SemaphoreType.DMA((9,)),
+            pltpu.SemaphoreType.DMA((9,)),
+        ],
+        compiler_params=pltpu.CompilerParams(
+            collective_id=1, has_side_effects=True, vmem_limit_bytes=48 * 1024 * 1024
+        ),
+    )(velocity, density)
 
 
 def halves(value):
@@ -96,6 +293,10 @@
         return jnp.dot(one, two, preferred_element_type=jnp.float32)
 
     return dot(left_big, right_big) + (dot(left_big, right_rest) + dot(left_rest, right_big))
+
+
+def dot_full(left, right):
+    return jnp.dot(left, right, precision=highest, preferred_element_type=jnp.float32)
 
 
 def mode_tables(full_x, length_z, slab, groups, anchor_kz):
@@ -337,7 +538,7 @@
         pressure = gain * (decay * left[row] + behind)
         special = jnp.where(zero[top], flats[row] + offset_flat, pressure[top])
         pressures[row] = jnp.concatenate([special, pressure[8:]], axis=0)
-    back = dot_split(txt_ref[...], jnp.concatenate(pressures, axis=1))
+    back = dot_full(txt_ref[...], jnp.concatenate(pressures, axis=1))
     for target in range(count_x):
         for row in range(rows + 1):
             columns = slice(row * lanes, (row + 1) * lanes)
@@ -377,11 +578,11 @@
 
     table = tz_ref[...]
     field = jnp.concatenate(spread(recv_b), axis=0)
-    field = dot_split(field.reshape((block_y + 1) * block_x, length_z), table)
+    field = dot_full(field.reshape((block_y + 1) * block_x, length_z), table)
     field = field.reshape(block_y + 1, block_x, length_z)
     for group, part in enumerate(spread(recv_e)):
         edge[group * rows : group * rows + part.shape[0], :] = part
-    following = dot_split(edge[...], table)[:block_y]
+    following = dot_full(edge[...], table)[:block_y]
     middle = field[:block_y]
     last_x = lax.broadcasted_iota(jnp.int32, middle.shape, 1) == block_x - 1
     ahead_x = jnp.where(last_x, following[:, None, :], jnp.roll(middle, -1, axis=1))
@@ -457,68 +658,10 @@
 
 
 def per_device(velocity, density):
-    block_x, block_y, length_z = density.shape
-    count_x = lax.axis_size("gx")
-    count_y = lax.axis_size("gy")
-    full_x = block_x * count_x
-    full_y = block_y * count_y
-    anchor_x = lax.axis_index("gx") * block_x
-    anchor_y = lax.axis_index("gy") * block_y
-
-    def confine(fields, rim_width):
-        along_x = anchor_x - rim_width + jnp.arange(block_x + 2 * rim_width)
-        along_y = anchor_y - rim_width + jnp.arange(block_y + 2 * rim_width)
-        along_z = jnp.arange(length_z)
-        inside = ((along_x >= 0) & (along_x < full_x))[:, None, None] & (
-            (along_y >= 0) & (along_y < full_y)
-        )[None, :, None]
-        open_x = inside & (along_x < full_x - 1)[:, None, None]
-        open_y = inside & (along_y < full_y - 1)[None, :, None]
-        open_z = inside & (along_z < length_z - 1)[None, None, :]
-        return jnp.stack(
-            [fields[0] * open_x, fields[1] * open_y, fields[2] * open_z, fields[3] * inside]
-        )
-
-    fields = jnp.concatenate(
-        [velocity.astype(jnp.float32), density.astype(jnp.float32)[None]], axis=0
-    )
-    widened = advect_halo(fields, 2)
-    section_one = confine(fields + time_step * tendency_rim(widened), 0)
-    section_one = advect_halo(section_one, 3)
-    earlier = cropped(widened, 2, 1)
-    section_two = confine(
-        0.5 * earlier + 0.5 * (cropped(section_one, 3, 1) + time_step * tendency_rim(section_one)),
-        1,
-    )
-    smoke_now = section_two[3]
-    smoke_above = jnp.concatenate(
-        [smoke_now[:, :, 1:], jnp.zeros_like(smoke_now[:, :, :1])], axis=2
-    )
-    lifted = confine(
-        jnp.stack(
-            [
-                section_two[0],
-                section_two[1],
-                section_two[2] + time_step * buoyancy * 0.5 * (smoke_now + smoke_above),
-                smoke_now,
-            ]
-        ),
-        1,
-    )
-    interior = lifted[:, 1:-1, 1:-1, :]
-    below_z = jnp.concatenate(
-        [jnp.zeros_like(interior[2][:, :, :1]), interior[2][:, :, :-1]], axis=2
-    )
-    divergence = (
-        interior[0]
-        - lifted[0, :-2, 1:-1, :]
-        + (interior[1] - lifted[1, 1:-1, :-2, :])
-        + (interior[2] - below_z)
-    )
-    column = interior[3]
-    attenuation = extinction / full_x
+    lifted, column, divergence = advect(velocity, density)
+    attenuation = extinction / (density.shape[0] * lax.axis_size("gx"))
     running = jnp.cumsum(column, axis=0)
-    projected, before = pressure_solve(divergence, interior[:3], running[-1])
+    projected, before = pressure_solve(divergence, lifted, running[-1])
     optical = attenuation * (before[None] + running - column)
     emission = jnp.exp(-optical) * -jnp.expm1(-attenuation * column) / attenuation
     return (projected, emission)

time: 127 us -> 81.9 us (0.64)
  Pallas kernels: 33.2 us -> 74.9 us
  other arithmetic: 37.8 us -> 2.82 us
  waiting for transfers between devices: 31.4 us -> 0 us
  starting transfers between devices: 19.9 us -> 0 us
    pallas_call x0 -> x1, Pallas kernels: none -> 44.3 us  [advect(): pl.pallas_call(functools.partial(advect_kernel, count_x, count_y), out_sh...]
    ppermute x8 -> x0, waiting for transfers between devices: 31.4 us -> none  [the longest x4 23.2 us: padded_2(): lax.ppermute(lax.slice_in_dim(block, 0, width, axis=dim), axis, backward)]
    ppermute x8 -> x0, starting transfers between devices: 19.9 us -> none  [the longest x4 14.5 us: padded_2(): lax.ppermute(lax.slice_in_dim(block, block.shape[dim] - width, None, axis...]
    add x3 -> x0, other arithmetic: 19.1 us -> none  [the longest x1 9.98 us: per_device(): 0.5 * earlier]
    concatenate x6 -> x0, other arithmetic: 7.15 us -> none  [the longest x5 6.41 us: padded_2(): block = jnp.concatenate([low, block, high], axis=dim)]
    mul x4 -> x0, other arithmetic: 5.56 us -> none  [the longest x2 3.54 us: flux_terms(): jnp.maximum(speed_axis, 0.0) * lower_diff]
    pallas_call x1, Pallas kernels: 33.2 us -> 30.6 us  [pressure_solve(): pl.pallas_call(functools.partial(solve_kernel, count_x, count_y), out_sha...]
    convert_element_type x2 -> x0, other arithmetic: 1.39 us -> none  [the longest x1 1.31 us: per_device(): velocity.astype(jnp.float32)]
  transfers between devices with their start and end apart: 8 -> 0, of which waited for: 6 -> 0; matrix products, arithmetic and copies ran while one was open for 2% -> 0% of each run, Pallas kernels for 0% -> 0%
where the time goes in v2:
time: 81.9 us; the launch traced here: 81.7 us
  Pallas kernels  74.9 us (91%)
  local copies, waits for them, and re-layouts  3.25 us (4%)
  other arithmetic  2.82 us (3%)
    pallas_call x1, Pallas kernels, advect(): pl.pallas_call(functools.partial(advect_kernel, count_x, count_y), out_sh...  44.3 us
    pallas_call x1, Pallas kernels, pressure_solve(): pl.pallas_call(functools.partial(solve_kernel, count_x, count_y), out_sha...  30.6 us
    unnamed x13, local copies, waits for them, and re-layouts  3.24 us

profile of v2, /device:TPU:0, one launch (start us, length us, event | category | flops | bytes accessed | tf_op | source)
XLA Modules:
  0.0 81.7 jit_solution(16069554257161748954)
XLA Ops:
  0.6 0.0 copy-start.4
  0.6 0.0 copy-start.5
  0.8 0.1 and_select_fusion
  0.9 0.0 copy-start
  0.9 1.1 %copy-done = bf16[3,16,32,256]{3,2,1,0:T(8,128)(2,1)S(1)} copy-done((bf16[3,16,32,256]{3,2,1,0:T(8,128)(2,1)S(1)}, bf16[3,16,32,256]{3,2,1,0:T(8,128)(2,1)}, u32[]{:S(2)}) %copy-start) | copy-done | bytes 786456
  2.0 0.0 copy-start.1
  2.0 0.9 %copy-done.1 = bf16[16,32,256]{2,1,0:T(8,128)(2,1)S(1)} copy-done((bf16[16,32,256]{2,1,0:T(8,128)(2,1)S(1)}, bf16[16,32,256]{2,1,0:T(8,128)(2,1)}, u32[]{:S(2)}) %copy-start.1) | copy-done | bytes 262168
  3.0 0.0 copy-start.2
  3.0 0.0 copy-start.3
  3.0 44.3 %shard_map.77 = (f32[3,16,32,256]{3,2,1,0:T(8,128)S(1)}, f32[16,32,256]{2,1,0:T(8,128)S(1)}, f32[16,32,256]{2,1,0:T(8,128)S(1)}) custom-call(bf16[3,16,32,256]{3,2,1,0:T(8,128)(2,1)S(1)} %copy-done, bf16[16,32,256]{2,1,0:T(8,128)(2,1)S(1)} %copy-done.1), custom_call_target="tpu_custom_call" | custom-call | tf_op jit(solution)/shard_map/pallas_call | solution.py:260
  47.3 1.5 %fusion.8 = f32[16,32,256]{2,1,0:T(8,128)S(1)} fusion(f32[16,32,256]{2,1,0:T(8,128)S(1)} %get-tuple-element.9), kind=kOutput, calls=%fused_computation.20 | output fusion | flops 1966080 | bytes 1048576 | tf_op jit(solution)/shard_map/jit(cumsum)/reduce_window_sum | solution.py:663
  48.9 0.0 copy-done.4
  48.9 0.0 copy-done.5
  48.9 0.0 copy-done.2
  48.9 0.0 copy-done.3
  48.9 30.6 %shard_map.78 = (f32[3,16,32,256]{3,2,1,0:T(8,128)S(1)}, f32[32,256]{1,0:T(8,128)S(1)}) custom-call(f32[16,32,256]{2,1,0:T(8,128)S(1)} %get-tuple-element.7.div_ref, f32[3,16,32,256]{3,2,1,0:T(8,128)S(1)} %get-tuple-element.8.lifted_ref, f32[32,256]{1,0:T(8,128)S(1)} %slice_bitcast_fusion.total_ref, f32[256,256]{1,0:T(8,128)S(1)} %copy-done.3, ...), custom_call_target="tpu_custom_call" | custom-call | tf_op jit(solution)/shard_map/pallas_call | solution.py:622
  79.5 1.1 %multiply_multiply_fusion = f32[16,32,256]{2,1,0:T(8,128)} fusion(f32[16,32,256]{2,1,0:T(8,128)S(1)} %get-tuple-element.9, f32[16,32,256]{2,1,0:T(8,128)S(1)} %fusion.8, f32[32,256]{1,0:T(8,128)S(1)} %get-tuple-element.11), kind=kLoop, calls=%fused_computation | loop fusion | flops 1048576 | bytes 1605632 | tf_op jit(solution)/shard_map/div | solution.py:666
  80.6 1.1 %copy.9 = f32[3,16,32,256]{3,2,1,0:T(8,128)} copy(f32[3,16,32,256]{3,2,1,0:T(8,128)S(1)} %get-tuple-element.16) | data formatting | bytes 3145728
  (5 shorter events, 0.1 us)
Async XLA Ops:
  0.6 48.2 %copy-start.4 = (f32[64,64]{1,0:T(8,128)S(1)}, f32[64,64]{1,0:T(8,128)}, u32[]{:S(2)}) copy-start(f32[64,64]{1,0:T(8,128)} %constant.61.clone.txt_ref) | copy-start | bytes 49156
  0.6 48.2 %copy-start.5 = (f32[64,64]{1,0:T(8,128)S(1)}, f32[64,64]{1,0:T(8,128)}, u32[]{:S(2)}) copy-start(f32[64,64]{1,0:T(8,128)} %constant.60.clone.tx_ref) | copy-start | bytes 49156
  0.9 1.1 %copy-start = (bf16[3,16,32,256]{3,2,1,0:T(8,128)(2,1)S(1)}, bf16[3,16,32,256]{3,2,1,0:T(8,128)(2,1)}, u32[]{:S(2)}) copy-start(bf16[3,16,32,256]{3,2,1,0:T(8,128)(2,1)} %velocity_ref.1) | copy-start | bytes 2359300
  2.0 0.9 %copy-start.1 = (bf16[16,32,256]{2,1,0:T(8,128)(2,1)S(1)}, bf16[16,32,256]{2,1,0:T(8,128)(2,1)}, u32[]{:S(2)}) copy-start(bf16[16,32,256]{2,1,0:T(8,128)(2,1)} %density_ref.1) | copy-start | bytes 786436
  3.0 45.9 %copy-start.2 = (f32[256,256]{1,0:T(8,128)S(1)}, f32[256,256]{1,0:T(8,128)}, u32[]{:S(2)}) copy-start(f32[256,256]{1,0:T(8,128)} %constant.59.clone.tzt_ref) | copy-start | bytes 786436
  3.0 45.9 %copy-start.3 = (f32[256,256]{1,0:T(8,128)S(1)}, f32[256,256]{1,0:T(8,128)}, u32[]{:S(2)}) copy-start(f32[256,256]{1,0:T(8,128)} %constant.58.clone.tz_ref) | copy-start | bytes 786436

commit v3 on v2

--- a/solution.py
+++ b/solution.py
@@ -21,9 +21,10 @@
     return (factor * np.cos(np.pi * modes * centres / length)).astype(np.float32)
 
 
-def advect_kernel(
+def advect_part(
     count_x,
     count_y,
+    meet,
     velocity_ref,
     density_ref,
     lifted_ref,
@@ -42,17 +43,26 @@
     last_x = block_x * count_x - 1
     last_y = block_y * count_y - 1
     low_y, high_y, rim = 16, 16 + block_y, 8
+    full = (low_y, low_y, block_y)
+    upward = (high_y - rim, low_y - rim, rim)
+    downward = (low_y, high_y, rim)
     moves = (
-        (1, 0, (0, 4), (block_x + 1, 1, 4), (low_y, low_y, block_y)),
-        (1, 0, (0, 1), (block_x, 0, 1), (low_y, low_y, block_y)),
-        (-1, 0, (0, 4), (5, block_x + 5, 4), (low_y, low_y, block_y)),
-        (1, 1, (0, 4), (block_x + 1, 1, 4), (high_y - rim, low_y - rim, rim)),
-        (1, -1, (0, 4), (block_x + 1, 1, 4), (low_y, high_y, rim)),
-        (-1, 1, (0, 4), (5, block_x + 5, 4), (high_y - rim, low_y - rim, rim)),
-        (-1, -1, (0, 4), (5, block_x + 5, 4), (low_y, high_y, rim)),
-        (0, 1, (0, 4), (5, 5, block_x), (high_y - rim, low_y - rim, rim)),
-        (0, -1, (0, 4), (5, 5, block_x), (low_y, high_y, rim)),
+        (1, 0, (0, 4), (block_x, 0, 2), full),
+        (-1, 0, (0, 4), (2, block_x + 2, 2), full),
+        (0, 1, (0, 4), (2, 2, block_x), upward),
+        (0, -1, (0, 4), (2, 2, block_x), downward),
+        (1, 0, (0, 4), (block_x + 1, 1, 2), full),
+        (-1, 0, (0, 4), (3, block_x + 3, 2), full),
+        (1, 0, (0, 1), (block_x, 0, 1), full),
+        (1, 1, (0, 2), (block_x + 1, 1, 2), upward),
+        (1, -1, (0, 1), (block_x + 2, 2, 1), downward),
+        (-1, 1, (1, 1), (3, block_x + 3, 2), upward),
+        (0, 1, (0, 4), (3, 3, block_x), upward),
+        (0, -1, (0, 4), (3, 3, block_x), downward),
     )
+
+    def array_of(index):
+        return wide if index < 4 else middle
 
     def exists(offset_x, offset_y):
         to_x = me_x + offset_x
@@ -62,10 +72,10 @@
     def copy_of(index):
         offset_x, offset_y, fields, along_x, along_y = moves[index]
         return pltpu.make_async_remote_copy(
-            src_ref=wide.at[
+            src_ref=array_of(index).at[
                 pl.ds(*fields), pl.ds(along_x[0], along_x[2]), pl.ds(along_y[0], along_y[2])
             ],
-            dst_ref=wide.at[
+            dst_ref=array_of(index).at[
                 pl.ds(*fields), pl.ds(along_x[1], along_x[2]), pl.ds(along_y[1], along_y[2])
             ],
             send_sem=sent.at[index],
@@ -74,40 +84,27 @@
             device_id_type=pl.DeviceIdType.MESH,
         )
 
-    around = [(i, j) for i in (-1, 0, 1) for j in (-1, 0, 1) if (i, j) != (0, 0)]
-    barrier = pltpu.get_barrier_semaphore()
-    for offset_x, offset_y in around:
-
-        @pl.when(exists(offset_x, offset_y))
-        def _():
-            pl.semaphore_signal(
-                barrier,
-                inc=1,
-                device_id={"gx": me_x + offset_x, "gy": me_y + offset_y},
-                device_id_type=pl.DeviceIdType.MESH,
-            )
-
     for field in range(3):
-        wide[field, 5 : 5 + block_x, low_y:high_y, :] = velocity_ref[field].astype(jnp.float32)
-    wide[3, 5 : 5 + block_x, low_y:high_y, :] = density_ref[...].astype(jnp.float32)
-    span_x = 3 - (me_x == 0).astype(jnp.int32) - (me_x == count_x - 1).astype(jnp.int32)
-    span_y = 3 - (me_y == 0).astype(jnp.int32) - (me_y == count_y - 1).astype(jnp.int32)
-    pl.semaphore_wait(barrier, span_x * span_y - 1)
-
-    for index, move in enumerate(moves):
-
-        @pl.when(exists(move[0], move[1]))
-        def _():
-            copy_of(index).start()
-
+        wide[field, 2 : 2 + block_x, low_y:high_y, :] = velocity_ref[field].astype(jnp.float32)
+    wide[3, 2 : 2 + block_x, low_y:high_y, :] = density_ref[...].astype(jnp.float32)
+    meet()
+
+    def depart(indices):
+        for index in indices:
+
+            @pl.when(exists(moves[index][0], moves[index][1]))
+            def _():
+                copy_of(index).start()
+
+    depart(range(4))
     for index, move in enumerate(moves):
         fields, along_x, along_y = move[2:]
 
         @pl.when(jnp.logical_not(exists(-move[0], -move[1])))
         def _():
             shape = (fields[1], along_x[2], along_y[2], length_z)
-            wide[
-                0 : fields[1],
+            array_of(index)[
+                fields[0] : fields[0] + fields[1],
                 along_x[1] : along_x[1] + along_x[2],
                 along_y[1] : along_y[1] + along_y[2],
                 :,
@@ -167,34 +164,33 @@
             return jnp.where(lane == length_z - 1, 0.0, value)
         return value
 
-    def first_rows(start, stop, fields=(0, 1, 2, 3), tiles=None):
-        tiles = range(low_y - rim, high_y + rim, 8) if tiles is None else tiles
-
-        def row(at, carry):
+    inside = tuple(range(low_y, high_y, 8))
+
+    def first_rows(start, stop, tiles=inside):
+        def row(at_x, carry):
             for at_y in tiles:
-                values = advance(wide, at + 2, at_y, fields)
-                for field, value in zip(fields, values):
-                    middle[field, at, at_y : at_y + 8, :] = walled(
-                        field, value, at - 3, at_y - low_y
+                values = advance(wide, at_x + 2, at_y, (0, 1, 2, 3))
+                for field, value in enumerate(values):
+                    middle[field, at_x + 3, at_y : at_y + 8, :] = walled(
+                        field, value, at_x, at_y - low_y
                     )
             return carry
 
-        lax.fori_loop(start + 3, stop + 3, row, 0)
+        lax.fori_loop(start, stop, row, 0)
 
     def second(at_x, at_y, fields):
         values = advance(middle, at_x + 3, at_y, fields)
         return [
-            0.5 * wide[field, at_x + 5, at_y : at_y + 8, :] + 0.5 * value
+            0.5 * wide[field, at_x + 2, at_y : at_y + 8, :] + 0.5 * value
             for field, value in zip(fields, values)
         ]
 
-    inside = range(low_y, high_y, 8)
-
-    def second_rows(start, stop):
+    def second_rows(start, stop, tiles=inside):
         def row(at_x, carry):
-            (value,) = second(at_x, low_y - 8, (1,))
-            face_y[at_x, 0:8, :] = walled(1, value, at_x, -8)
-            for at_y in inside:
+            if inside[0] in tiles:
+                (value,) = second(at_x, low_y - 8, (1,))
+                face_y[at_x, 0:8, :] = walled(1, value, at_x, -8)
+            for at_y in tiles:
                 near = at_y - low_y
                 part_x, part_y, part_z, smoke = second(at_x, at_y, (0, 1, 2, 3))
                 above = pltpu.roll(smoke, length_z - 1, 1)
@@ -207,18 +203,23 @@
 
         lax.fori_loop(start, stop, row, 0)
 
-    arrive((7, 8))
-    first_rows(2, block_x - 2)
-    second_rows(4, block_x - 4)
-    arrive(range(7))
-    first_rows(-3, -2, (0,), inside)
-    first_rows(-2, 2)
-    first_rows(block_x - 2, block_x + 2)
+    rims = (inside[0], inside[-1])
+    first_rows(2, block_x - 2, inside[1:-1])
+    arrive((2, 3))
+    first_rows(2, block_x - 2, rims)
+    arrive((0, 1))
+    first_rows(0, 2)
+    first_rows(block_x - 2, block_x)
+    depart(range(4, 12))
+    second_rows(2, block_x - 2, inside[1:-1])
+    arrive((10, 11))
+    second_rows(2, block_x - 2, rims)
+    arrive(range(4, 10))
     for at_y in inside:
         (value,) = second(-1, at_y, (0,))
         face_x[0, at_y - low_y : at_y - low_y + 8, :] = walled(0, value, -1, 0)
-    second_rows(0, 4)
-    second_rows(block_x - 4, block_x)
+    second_rows(0, 2)
+    second_rows(block_x - 2, block_x)
 
     def differ(at_x, carry):
         part_x = face_x[at_x + 1]
@@ -243,41 +244,6 @@
         @pl.when(exists(move[0], move[1]))
         def _():
             copy_of(index).wait_send()
-
-
-def advect(velocity, density):
-    block_x, block_y, length_z = density.shape
-    count_x = lax.axis_size("gx")
-    count_y = lax.axis_size("gy")
-    vmem = pl.BlockSpec(memory_space=pltpu.VMEM)
-
-    def buffer(*shape):
-        return pltpu.VMEM(shape, jnp.float32)
-
-    def result(*shape):
-        return jax.ShapeDtypeStruct(shape, jnp.float32)
-
-    return pl.pallas_call(
-        functools.partial(advect_kernel, count_x, count_y),
-        out_shape=(
-            result(3, *density.shape),
-            result(*density.shape),
-            result(*density.shape),
-        ),
-        in_specs=[vmem] * 2,
-        out_specs=(vmem,) * 3,
-        scratch_shapes=[
-            buffer(4, block_x + 9, block_y + 32, length_z),
-            buffer(4, block_x + 5, block_y + 32, length_z),
-            buffer(block_x + 1, block_y, length_z),
-            buffer(block_x, block_y + 8, length_z),
-            pltpu.SemaphoreType.DMA((9,)),
-            pltpu.SemaphoreType.DMA((9,)),
-        ],
-        compiler_params=pltpu.CompilerParams(
-            collective_id=1, has_side_effects=True, vmem_limit_bytes=48 * 1024 * 1024
-        ),
-    )(velocity, density)
 
 
 def halves(value):
@@ -313,7 +279,7 @@
     return decay, gain
 
 
-def solve_kernel(
+def solve_part(
     count_x,
     count_y,
     div_ref,
@@ -326,7 +292,8 @@
     decay_ref,
     gain_ref,
     out_ref,
-    before_ref,
+    emission_ref,
+    smoke_ref,
     send_a,
     recv_a,
     send_b,
@@ -349,41 +316,24 @@
     groups = lanes // slab
     rows = block_y // groups
 
-    barrier = pltpu.get_barrier_semaphore()
-    for offset in range(1, count_x):
-        pl.semaphore_signal(
-            barrier,
-            inc=1,
-            device_id={"gx": lax.rem(me_x + offset, count_x)},
-            device_id_type=pl.DeviceIdType.MESH,
-        )
-    for offset in range(1, count_y):
-        pl.semaphore_signal(
-            barrier,
-            inc=1,
-            device_id={"gy": lax.rem(me_y + offset, count_y)},
-            device_id_type=pl.DeviceIdType.MESH,
-        )
-    div = jnp.swapaxes(div_ref[...], 0, 1).reshape(block_y * block_x, length_z)
-    along = dot_split(div, tzt_ref[...]).reshape(block_y, block_x, length_z)
-    for target in range(count_x):
-        send_a[target] = jnp.concatenate(
-            [
-                along[group * rows : (group + 1) * rows, :, target * slab : (target + 1) * slab]
-                for group in range(groups)
-            ],
-            axis=-1,
-        )
-    pl.semaphore_wait(barrier, count_x + count_y - 2)
-
-    def to_x(kind, source, target):
+    half = rows // 2
+    chunks = ((0, half), (half, rows))
+
+    def to_x(kind, source, target, start=None, stop=None):
         copies = []
         for offset in range(1, count_x):
             to = lax.rem(me_x + offset, count_x)
+            if source is total_ref:
+                source_at, target_at = source, target.at[me_x]
+            elif start is None:
+                source_at, target_at = source.at[to], target.at[me_x]
+            else:
+                source_at = source.at[to, pl.ds(start, stop - start)]
+                target_at = target.at[me_x, pl.ds(start, stop - start)]
             copies.append(
                 pltpu.make_async_remote_copy(
-                    src_ref=source.at[to] if source is not total_ref else source,
-                    dst_ref=target.at[me_x],
+                    src_ref=source_at,
+                    dst_ref=target_at,
                     send_sem=sems_x.at[kind, 0, offset],
                     recv_sem=sems_x.at[kind, 1, offset],
                     device_id={"gx": to},
@@ -394,8 +344,29 @@
             copy.start()
         return copies
 
-    copies_a = to_x(0, send_a, recv_a)
-    copies_t = to_x(1, total_ref, totals)
+    table = tzt_ref[...]
+    copies_a = []
+    for kind, (start, stop) in enumerate(chunks):
+        size = stop - start
+        div = jnp.concatenate(
+            [
+                jnp.swapaxes(div_ref[:, group * rows + start : group * rows + stop, :], 0, 1)
+                for group in range(groups)
+            ],
+            axis=0,
+        )
+        along = dot_split(div.reshape(groups * size * block_x, length_z), table)
+        along = along.reshape(groups, size, block_x, length_z)
+        for target in range(count_x):
+            send_a[target, start:stop] = jnp.concatenate(
+                [
+                    along[group, :, :, target * slab : (target + 1) * slab]
+                    for group in range(groups)
+                ],
+                axis=-1,
+            )
+        copies_a.append(to_x(kind, send_a, recv_a, start, stop))
+    copies_t = to_x(2, total_ref, totals)
     recv_a[me_x] = send_a[me_x]
 
     lane = lax.broadcasted_iota(jnp.int32, (full_x, lanes), 1)
@@ -424,18 +395,19 @@
     decay_block = power(decay_rows, groups)
     decay_full = power(decay_block, count_y)
 
-    for copy in copies_a:
-        copy.wait()
-    gathered = jnp.concatenate(
-        [
-            jnp.concatenate([recv_a[place, row] for place in range(count_x)], axis=0)
-            for row in range(rows)
-        ],
-        axis=1,
-    )
-    modes = dot_split(tx_ref[...], gathered)
-    for row in range(rows):
-        hat[row] = modes[:, row * lanes : (row + 1) * lanes]
+    for copies, (start, stop) in zip(copies_a, chunks):
+        for copy in copies:
+            copy.wait()
+        gathered = jnp.concatenate(
+            [
+                jnp.concatenate([recv_a[place, row] for place in range(count_x)], axis=0)
+                for row in range(start, stop)
+            ],
+            axis=1,
+        )
+        modes = dot_split(tx_ref[...], gathered)
+        for row in range(start, stop):
+            hat[row] = modes[:, (row - start) * lanes : (row - start + 1) * lanes]
 
     forward = hat[0]
     for row in range(1, rows):
@@ -548,61 +520,179 @@
                 send_e[target, row : row + 1, :] = back[after : after + 1, columns]
         if target == count_x - 1:
             send_e[target] = jnp.zeros(send_e.shape[1:], jnp.float32)
-    copies_b = to_x(2, send_b, recv_b)
     copies_e = to_x(3, send_e, recv_e)
+    copies_high = to_x(4, send_b, recv_b, half, rows + 1)
+    copies_low = to_x(5, send_b, recv_b, 0, half)
     recv_b[me_x] = send_b[me_x]
     recv_e[me_x] = send_e[me_x]
     for copy in copies_t:
         copy.wait()
-    before = jnp.zeros_like(before_ref)
+    running = jnp.zeros_like(total_ref)
     for place in range(count_x - 1):
-        before = jnp.where(place < me_x, before + totals[place], before)
-    before_ref[...] = before
-    for copy in copies_b + copies_e:
+        running = jnp.where(place < me_x, running + totals[place], running)
+    attenuation = extinction / full_x
+    for at_x in range(block_x):
+        column = smoke_ref[at_x]
+        thickness = attenuation * column
+        absorbed = jnp.tanh(0.5 * thickness) * (1.0 + jnp.exp(-thickness))
+        emission_ref[at_x] = jnp.exp(-attenuation * running) * absorbed * (1.0 / attenuation)
+        running = running + column
+
+    table_back = tz_ref[...]
+    for copy in copies_e:
         copy.wait()
-
-    def spread(ref):
-        parts = []
-        for group in range(groups):
-            size = rows + (group == groups - 1)
-            parts.append(
+    for group in range(groups):
+        size = rows + (group == groups - 1)
+        edge[group * rows : group * rows + size, :] = jnp.concatenate(
+            [
+                recv_e[place][:size, group * slab : (group + 1) * slab]
+                for place in range(count_x)
+            ],
+            axis=-1,
+        )
+    following = dot_full(edge[...], table_back)[:block_y]
+    after = None
+    for copies, (start, stop) in ((copies_high, (half, rows + 1)), (copies_low, (0, half))):
+        for copy in copies:
+            copy.wait()
+        size = stop - start
+        field = jnp.concatenate(
+            [
                 jnp.concatenate(
                     [
-                        ref[place][:size, ..., group * slab : (group + 1) * slab]
+                        recv_b[place, start:stop][..., group * slab : (group + 1) * slab]
                         for place in range(count_x)
                     ],
                     axis=-1,
                 )
+                for group in range(groups)
+            ],
+            axis=0,
+        )
+        field = dot_full(field.reshape(groups * size * block_x, length_z), table_back)
+        field = field.reshape(groups, size, block_x, length_z)
+        if after is not None:
+            field = jnp.concatenate([field, after], axis=1)
+        after = field[:, :1]
+        for group in range(groups):
+            middle = field[group, :half]
+            at_y = group * rows + start
+            shape = middle.shape
+            last_x = lax.broadcasted_iota(jnp.int32, shape, 1) == block_x - 1
+            ahead_x = jnp.where(
+                last_x, following[at_y : at_y + half][:, None, :], jnp.roll(middle, -1, axis=1)
             )
-        return parts
-
-    table = tz_ref[...]
-    field = jnp.concatenate(spread(recv_b), axis=0)
-    field = dot_full(field.reshape((block_y + 1) * block_x, length_z), table)
-    field = field.reshape(block_y + 1, block_x, length_z)
-    for group, part in enumerate(spread(recv_e)):
-        edge[group * rows : group * rows + part.shape[0], :] = part
-    following = dot_full(edge[...], table)[:block_y]
-    middle = field[:block_y]
-    last_x = lax.broadcasted_iota(jnp.int32, middle.shape, 1) == block_x - 1
-    ahead_x = jnp.where(last_x, following[:, None, :], jnp.roll(middle, -1, axis=1))
-    ahead_z = pltpu.roll(middle, length_z - 1, 2)
-    gradients = (ahead_x - middle, field[1:] - middle, ahead_z - middle)
-    place_x = lax.broadcasted_iota(jnp.int32, div_ref.shape, 0) + me_x * block_x
-    place_y = lax.broadcasted_iota(jnp.int32, div_ref.shape, 1) + me_y * block_y
-    place_z = lax.broadcasted_iota(jnp.int32, div_ref.shape, 2)
-    opened = (
-        place_x < full_x - 1,
-        place_y < block_y * count_y - 1,
-        place_z < length_z - 1,
+            ahead_z = pltpu.roll(middle, length_z - 1, 2)
+            gradients = (ahead_x - middle, field[group, 1 : half + 1] - middle, ahead_z - middle)
+            shape = (block_x, half, length_z)
+            opened = (
+                lax.broadcasted_iota(jnp.int32, shape, 0) + me_x * block_x < full_x - 1,
+                lax.broadcasted_iota(jnp.int32, shape, 1) + (me_y * block_y + at_y)
+                < block_y * count_y - 1,
+                lax.broadcasted_iota(jnp.int32, shape, 2) < length_z - 1,
+            )
+            for axis_id in range(3):
+                value = lifted_ref[axis_id, :, at_y : at_y + half, :] - jnp.swapaxes(
+                    gradients[axis_id], 0, 1
+                )
+                out_ref[axis_id, :, at_y : at_y + half, :] = jnp.where(
+                    opened[axis_id], value, 0.0
+                )
+
+
+def step_kernel(
+    count_x,
+    count_y,
+    velocity_ref,
+    density_ref,
+    tz_ref,
+    tzt_ref,
+    tx_ref,
+    txt_ref,
+    decay_ref,
+    gain_ref,
+    out_ref,
+    emission_ref,
+    wide,
+    middle,
+    face_x,
+    face_y,
+    sent,
+    received,
+    lifted,
+    smoke,
+    div,
+    total,
+    *rest,
+):
+    me_x = lax.axis_index("gx")
+    me_y = lax.axis_index("gy")
+    barrier = pltpu.get_barrier_semaphore()
+
+    def greet(to_x, to_y):
+        pl.semaphore_signal(
+            barrier,
+            inc=1,
+            device_id={"gx": to_x, "gy": to_y},
+            device_id_type=pl.DeviceIdType.MESH,
+        )
+
+    for offset in range(1, count_x):
+        greet(lax.rem(me_x + offset, count_x), me_y)
+    for offset in range(1, count_y):
+        greet(me_x, lax.rem(me_y + offset, count_y))
+    for offset_x in (-1, 1):
+        for offset_y in (-1, 1):
+            to_x = me_x + offset_x
+            to_y = me_y + offset_y
+
+            @pl.when((to_x >= 0) & (to_x < count_x) & (to_y >= 0) & (to_y < count_y))
+            def _():
+                greet(to_x, to_y)
+
+    def meet():
+        beside_x = 2 - (me_x == 0).astype(jnp.int32) - (me_x == count_x - 1).astype(jnp.int32)
+        beside_y = 2 - (me_y == 0).astype(jnp.int32) - (me_y == count_y - 1).astype(jnp.int32)
+        pl.semaphore_wait(barrier, count_x + count_y - 2 + beside_x * beside_y)
+
+    advect_part(
+        count_x,
+        count_y,
+        meet,
+        velocity_ref,
+        density_ref,
+        lifted,
+        smoke,
+        div,
+        wide,
+        middle,
+        face_x,
+        face_y,
+        sent,
+        received,
     )
-    for axis_id in range(3):
-        value = lifted_ref[axis_id] - jnp.swapaxes(gradients[axis_id], 0, 1)
-        out_ref[axis_id] = jnp.where(opened[axis_id], value, 0.0)
-
-
-def pressure_solve(divergence, lifted, total):
-    block_x, block_y, length_z = divergence.shape
+    total[...] = jnp.sum(smoke[...], axis=0)
+    solve_part(
+        count_x,
+        count_y,
+        div,
+        lifted,
+        total,
+        tz_ref,
+        tzt_ref,
+        tx_ref,
+        txt_ref,
+        decay_ref,
+        gain_ref,
+        out_ref,
+        emission_ref,
+        smoke,
+        *rest,
+    )
+
+
+def per_device(velocity, density):
+    block_x, block_y, length_z = density.shape
     count_x = lax.axis_size("gx")
     count_y = lax.axis_size("gy")
     full_x = block_x * count_x
@@ -620,14 +710,24 @@
         return pltpu.VMEM(shape, jnp.float32)
 
     return pl.pallas_call(
-        functools.partial(solve_kernel, count_x, count_y),
+        functools.partial(step_kernel, count_x, count_y),
         out_shape=(
-            jax.ShapeDtypeStruct(lifted.shape, jnp.float32),
-            jax.ShapeDtypeStruct(total.shape, jnp.float32),
+            jax.ShapeDtypeStruct(velocity.shape, jnp.float32),
+            jax.ShapeDtypeStruct(density.shape, jnp.float32),
         ),
-        in_specs=[vmem] * 9,
+        in_specs=[vmem] * 8,
         out_specs=(vmem, vmem),
         scratch_shapes=[
+            buffer(4, block_x + 4, block_y + 32, length_z),
+            buffer(4, block_x + 5, block_y + 32, length_z),
+            buffer(block_x + 1, block_y, length_z),
+            buffer(block_x, block_y + 8, length_z),
+            pltpu.SemaphoreType.DMA((12,)),
+            pltpu.SemaphoreType.DMA((12,)),
+            buffer(3, block_x, block_y, length_z),
+            buffer(block_x, block_y, length_z),
+            buffer(block_x, block_y, length_z),
+            buffer(block_y, length_z),
             buffer(count_x, rows, block_x, lanes),
             buffer(count_x, rows, block_x, lanes),
             buffer(count_x, rows + 1, block_x, lanes),
@@ -635,19 +735,18 @@
             buffer(count_x, padded, lanes),
             buffer(count_x, padded, lanes),
             buffer(block_y + 8, length_z),
-            buffer(count_x, *total.shape),
+            buffer(count_x, block_y, length_z),
             buffer(count_y, full_x, lanes),
             buffer(rows, full_x, lanes),
-            pltpu.SemaphoreType.DMA((4, 2, count_x)),
+            pltpu.SemaphoreType.DMA((6, 2, count_x)),
             pltpu.SemaphoreType.DMA((2, count_y)),
         ],
         compiler_params=pltpu.CompilerParams(
             collective_id=0, has_side_effects=True, vmem_limit_bytes=48 * 1024 * 1024
         ),
     )(
-        divergence,
-        lifted,
-        total,
+        velocity,
+        density,
         jnp.asarray(table_z),
         jnp.asarray(table_z.T.copy()),
         jnp.asarray(table_x),
@@ -657,16 +756,6 @@
     )
 
 
-def per_device(velocity, density):
-    lifted, column, divergence = advect(velocity, density)
-    attenuation = extinction / (density.shape[0] * lax.axis_size("gx"))
-    running = jnp.cumsum(column, axis=0)
-    projected, before = pressure_solve(divergence, lifted, running[-1])
-    optical = attenuation * (before[None] + running - column)
-    emission = jnp.exp(-optical) * -jnp.expm1(-attenuation * column) / attenuation
-    return (projected, emission)
-
-
 def solution(mesh):
     in_specs = (P(None, "gx", "gy", None), P("gx", "gy", None))
     out_specs = (P(None, "gx", "gy", None), P("gx", "gy", None))

time: 81.9 us -> 72.2 us (0.88)
  Pallas kernels: 74.9 us -> 63.5 us
  local copies, waits for them, and re-layouts: 3.25 us -> 7.43 us
  other arithmetic: 2.82 us -> 0.21 us
    pallas_call x2 -> x1, Pallas kernels: 74.9 us -> 63.5 us  [per_device(): pl.pallas_call(functools.partial(step_kernel, count_x, count_y), out_shap...]
    unnamed x13 -> x14, local copies, waits for them, and re-layouts: 3.24 us -> 7.43 us
    another operation x1 -> x0, other arithmetic: 1.52 us -> none  [per_device(): running = jnp.cumsum(column, axis=0)]
    div x1 -> x0, other arithmetic: 1.09 us -> none  [per_device(): jnp.exp(-optical) * -jnp.expm1(-attenuation * column) / attenuation]
where the time goes in v3:
time: 72.2 us; the launch traced here: 71.8 us
  Pallas kernels  63.5 us (88%)
  local copies, waits for them, and re-layouts  7.43 us (10%)
    pallas_call x1, Pallas kernels, per_device(): pl.pallas_call(functools.partial(step_kernel, count_x, count_y), out_shap...  63.5 us
    unnamed x14, local copies, waits for them, and re-layouts  7.43 us

profile of v3, /device:TPU:0, one launch (start us, length us, event | category | flops | bytes accessed | tf_op | source)
XLA Modules:
  0.0 71.8 jit_solution(1824548266949528064)
XLA Ops:
  0.8 0.1 and_select_fusion
  0.9 0.0 copy-start
  0.9 1.1 %copy-done = bf16[3,16,32,256]{3,2,1,0:T(8,128)(2,1)S(1)} copy-done((bf16[3,16,32,256]{3,2,1,0:T(8,128)(2,1)S(1)}, bf16[3,16,32,256]{3,2,1,0:T(8,128)(2,1)}, u32[]{:S(2)}) %copy-start) | copy-done | bytes 786456
  2.0 0.0 copy-start.1
  2.0 0.9 %copy-done.1 = bf16[16,32,256]{2,1,0:T(8,128)(2,1)S(1)} copy-done((bf16[16,32,256]{2,1,0:T(8,128)(2,1)S(1)}, bf16[16,32,256]{2,1,0:T(8,128)(2,1)}, u32[]{:S(2)}) %copy-start.1) | copy-done | bytes 262168
  3.0 0.0 copy-start.2
  3.0 0.9 %copy-done.2 = f32[256,256]{1,0:T(8,128)S(1)} copy-done((f32[256,256]{1,0:T(8,128)S(1)}, f32[256,256]{1,0:T(8,128)}, u32[]{:S(2)}) %copy-start.2) | copy-done | bytes 262168
  3.9 0.0 copy-start.3
  3.9 0.9 %copy-done.3 = f32[256,256]{1,0:T(8,128)S(1)} copy-done((f32[256,256]{1,0:T(8,128)S(1)}, f32[256,256]{1,0:T(8,128)}, u32[]{:S(2)}) %copy-start.3) | copy-done | bytes 262168
  4.9 0.0 copy-start.4
  4.9 0.8 %copy-done.4 = f32[64,64]{1,0:T(8,128)S(1)} copy-done((f32[64,64]{1,0:T(8,128)S(1)}, f32[64,64]{1,0:T(8,128)}, u32[]{:S(2)}) %copy-start.4) | copy-done | bytes 16408
  5.6 0.0 copy-start.5
  5.6 0.8 %copy-done.5 = f32[64,64]{1,0:T(8,128)S(1)} copy-done((f32[64,64]{1,0:T(8,128)S(1)}, f32[64,64]{1,0:T(8,128)}, u32[]{:S(2)}) %copy-start.5) | copy-done | bytes 16408
  6.4 63.5 %shard_map.77 = (f32[3,16,32,256]{3,2,1,0:T(8,128)S(1)}, f32[16,32,256]{2,1,0:T(8,128)S(1)}) custom-call(bf16[3,16,32,256]{3,2,1,0:T(8,128)(2,1)S(1)} %copy-done, bf16[16,32,256]{2,1,0:T(8,128)(2,1)S(1)} %copy-done.1, f32[256,256]{1,0:T(8,128)S(1)} %copy-done.3, f32[256,256]{1,0:T(8,128)S(1)} %copy-done.2, f32[64,64]{1,0:T(8,128)S(1)} %copy-done.5, ...), custom_call_target="tpu_custom_call" | custom-call | tf_op jit(solution)/shard_map/pallas_call | solution.py:712
  69.9 1.1 %copy.10 = f32[3,16,32,256]{3,2,1,0:T(8,128)} copy(f32[3,16,32,256]{3,2,1,0:T(8,128)S(1)} %get-tuple-element.6) | data formatting | bytes 3145728
  71.0 0.8 %copy.11 = f32[16,32,256]{2,1,0:T(8,128)} copy(f32[16,32,256]{2,1,0:T(8,128)S(1)} %get-tuple-element.7) | data formatting | bytes 1048576
  (4 shorter events, 0.1 us)
Async XLA Ops:
  0.9 1.1 %copy-start = (bf16[3,16,32,256]{3,2,1,0:T(8,128)(2,1)S(1)}, bf16[3,16,32,256]{3,2,1,0:T(8,128)(2,1)}, u32[]{:S(2)}) copy-start(bf16[3,16,32,256]{3,2,1,0:T(8,128)(2,1)} %velocity_ref.1) | copy-start | bytes 2359300
  2.0 0.9 %copy-start.1 = (bf16[16,32,256]{2,1,0:T(8,128)(2,1)S(1)}, bf16[16,32,256]{2,1,0:T(8,128)(2,1)}, u32[]{:S(2)}) copy-start(bf16[16,32,256]{2,1,0:T(8,128)(2,1)} %density_ref.1) | copy-start | bytes 786436
  3.0 0.9 %copy-start.2 = (f32[256,256]{1,0:T(8,128)S(1)}, f32[256,256]{1,0:T(8,128)}, u32[]{:S(2)}) copy-start(f32[256,256]{1,0:T(8,128)} %constant.50.clone.tzt_ref) | copy-start | bytes 786436
  3.9 0.9 %copy-start.3 = (f32[256,256]{1,0:T(8,128)S(1)}, f32[256,256]{1,0:T(8,128)}, u32[]{:S(2)}) copy-start(f32[256,256]{1,0:T(8,128)} %constant.49.clone.tz_ref) | copy-start | bytes 786436
  4.9 0.8 %copy-start.4 = (f32[64,64]{1,0:T(8,128)S(1)}, f32[64,64]{1,0:T(8,128)}, u32[]{:S(2)}) copy-start(f32[64,64]{1,0:T(8,128)} %constant.52.clone.txt_ref) | copy-start | bytes 49156
  5.6 0.8 %copy-start.5 = (f32[64,64]{1,0:T(8,128)S(1)}, f32[64,64]{1,0:T(8,128)}, u32[]{:S(2)}) copy-start(f32[64,64]{1,0:T(8,128)} %constant.51.clone.tx_ref) | copy-start | bytes 49156

commit v4 on v3

--- a/solution.py
+++ b/solution.py
@@ -43,26 +43,42 @@
     last_x = block_x * count_x - 1
     last_y = block_y * count_y - 1
     low_y, high_y, rim = 16, 16 + block_y, 8
-    full = (low_y, low_y, block_y)
+    half = block_y // 2
+    parts = tuple((start, start, half) for start in (low_y, low_y + half))
     upward = (high_y - rim, low_y - rim, rim)
     downward = (low_y, high_y, rim)
-    moves = (
-        (1, 0, (0, 4), (block_x, 0, 2), full),
-        (-1, 0, (0, 4), (2, block_x + 2, 2), full),
+    first_x = [
+        [(1, 0, (0, 4), (block_x, 0, 2), part), (-1, 0, (0, 4), (2, block_x + 2, 2), part)]
+        for part in parts
+    ]
+    first_y = [
         (0, 1, (0, 4), (2, 2, block_x), upward),
         (0, -1, (0, 4), (2, 2, block_x), downward),
-        (1, 0, (0, 4), (block_x + 1, 1, 2), full),
-        (-1, 0, (0, 4), (3, block_x + 3, 2), full),
-        (1, 0, (0, 1), (block_x, 0, 1), full),
-        (1, 1, (0, 2), (block_x + 1, 1, 2), upward),
-        (1, -1, (0, 1), (block_x + 2, 2, 1), downward),
-        (-1, 1, (1, 1), (3, block_x + 3, 2), upward),
+    ]
+    second_x = [
+        [
+            (1, 0, (0, 4), (block_x + 1, 1, 2), part),
+            (-1, 0, (0, 4), (3, block_x + 3, 2), part),
+            (1, 0, (0, 1), (block_x, 0, 1), part),
+        ]
+        for part in parts
+    ]
+    second_x[0].append((1, -1, (0, 1), (block_x + 2, 2, 1), downward))
+    second_x[1].append((1, 1, (0, 2), (block_x + 1, 1, 2), upward))
+    second_x[1].append((-1, 1, (1, 1), (3, block_x + 3, 2), upward))
+    second_y = [
         (0, 1, (0, 4), (3, 3, block_x), upward),
         (0, -1, (0, 4), (3, 3, block_x), downward),
-    )
+    ]
+    groups = (first_x[0], first_y, first_x[1], second_x[0], second_x[1], second_y)
+    moves = [move for group in groups for move in group]
+    spans = []
+    for group in groups:
+        begin = spans[-1].stop if spans else 0
+        spans.append(range(begin, begin + len(group)))
 
     def array_of(index):
-        return wide if index < 4 else middle
+        return wide if index < spans[3].start else middle
 
     def exists(offset_x, offset_y):
         to_x = me_x + offset_x
@@ -96,7 +112,7 @@
             def _():
                 copy_of(index).start()
 
-    depart(range(4))
+    depart(range(spans[3].start))
     for index, move in enumerate(moves):
         fields, along_x, along_y = move[2:]
 
@@ -205,16 +221,19 @@
 
     rims = (inside[0], inside[-1])
     first_rows(2, block_x - 2, inside[1:-1])
-    arrive((2, 3))
+    arrive(spans[1])
     first_rows(2, block_x - 2, rims)
-    arrive((0, 1))
-    first_rows(0, 2)
-    first_rows(block_x - 2, block_x)
-    depart(range(4, 12))
+    for part in range(2):
+        lines = inside[part * len(inside) // 2 : (part + 1) * len(inside) // 2]
+        arrive(spans[2 * part])
+        first_rows(0, 2, lines)
+        first_rows(block_x - 2, block_x, lines)
+        depart(spans[3 + part])
+    depart(spans[5])
     second_rows(2, block_x - 2, inside[1:-1])
-    arrive((10, 11))
+    arrive(spans[5])
     second_rows(2, block_x - 2, rims)
-    arrive(range(4, 10))
+    arrive([*spans[3], *spans[4]])
     for at_y in inside:
         (value,) = second(-1, at_y, (0,))
         face_x[0, at_y - low_y : at_y - low_y + 8, :] = walled(0, value, -1, 0)
@@ -575,26 +594,22 @@
             field = jnp.concatenate([field, after], axis=1)
         after = field[:, :1]
         for group in range(groups):
-            middle = field[group, :half]
             at_y = group * rows + start
+            middle = jnp.swapaxes(field[group, :half], 0, 1)
+            ahead_x = jnp.concatenate([middle[1:], following[None, at_y : at_y + half]], axis=0)
             shape = middle.shape
-            last_x = lax.broadcasted_iota(jnp.int32, shape, 1) == block_x - 1
-            ahead_x = jnp.where(
-                last_x, following[at_y : at_y + half][:, None, :], jnp.roll(middle, -1, axis=1)
+            line = lax.broadcasted_iota(jnp.int32, shape, 1)
+            ahead_y = jnp.where(
+                line == half - 1, field[group, half][:, None, :], jnp.roll(middle, -1, axis=1)
             )
             ahead_z = pltpu.roll(middle, length_z - 1, 2)
-            gradients = (ahead_x - middle, field[group, 1 : half + 1] - middle, ahead_z - middle)
-            shape = (block_x, half, length_z)
             opened = (
                 lax.broadcasted_iota(jnp.int32, shape, 0) + me_x * block_x < full_x - 1,
-                lax.broadcasted_iota(jnp.int32, shape, 1) + (me_y * block_y + at_y)
-                < block_y * count_y - 1,
+                line + (me_y * block_y + at_y) < block_y * count_y - 1,
                 lax.broadcasted_iota(jnp.int32, shape, 2) < length_z - 1,
             )
-            for axis_id in range(3):
-                value = lifted_ref[axis_id, :, at_y : at_y + half, :] - jnp.swapaxes(
-                    gradients[axis_id], 0, 1
-                )
+            for axis_id, ahead in enumerate((ahead_x, ahead_y, ahead_z)):
+                value = lifted_ref[axis_id, :, at_y : at_y + half, :] - (ahead - middle)
                 out_ref[axis_id, :, at_y : at_y + half, :] = jnp.where(
                     opened[axis_id], value, 0.0
                 )
@@ -627,6 +642,15 @@
 ):
     me_x = lax.axis_index("gx")
     me_y = lax.axis_index("gy")
+    *rest, fetched = rest
+    given = (velocity_ref, density_ref, tz_ref, tzt_ref, tx_ref, txt_ref, decay_ref, gain_ref)
+    held, rest = rest[-len(given) :], rest[: -len(given)]
+    fetches = [
+        pltpu.make_async_copy(source, target, fetched.at[index])
+        for index, (source, target) in enumerate(zip(given, held))
+    ]
+    for fetch in fetches:
+        fetch.start()
     barrier = pltpu.get_barrier_semaphore()
 
     def greet(to_x, to_y):
@@ -655,12 +679,13 @@
         beside_y = 2 - (me_y == 0).astype(jnp.int32) - (me_y == count_y - 1).astype(jnp.int32)
         pl.semaphore_wait(barrier, count_x + count_y - 2 + beside_x * beside_y)
 
+    for fetch in fetches[:2]:
+        fetch.wait()
     advect_part(
         count_x,
         count_y,
         meet,
-        velocity_ref,
-        density_ref,
+        *held[:2],
         lifted,
         smoke,
         div,
@@ -672,18 +697,15 @@
         received,
     )
     total[...] = jnp.sum(smoke[...], axis=0)
+    for fetch in fetches[2:]:
+        fetch.wait()
     solve_part(
         count_x,
         count_y,
         div,
         lifted,
         total,
-        tz_ref,
-        tzt_ref,
-        tx_ref,
-        txt_ref,
-        decay_ref,
-        gain_ref,
+        *held[2:],
         out_ref,
         emission_ref,
         smoke,
@@ -704,6 +726,16 @@
     table_z = cosine_table(length_z)
     table_x = cosine_table(full_x)
     decay, gain = mode_tables(full_x, length_z, slab, groups, lax.axis_index("gx") * slab)
+    operands = (
+        velocity,
+        density,
+        jnp.asarray(table_z),
+        jnp.asarray(table_z.T.copy()),
+        jnp.asarray(table_x),
+        jnp.asarray(table_x.T.copy()),
+        decay,
+        gain,
+    )
     vmem = pl.BlockSpec(memory_space=pltpu.VMEM)
 
     def buffer(*shape):
@@ -715,15 +747,15 @@
             jax.ShapeDtypeStruct(velocity.shape, jnp.float32),
             jax.ShapeDtypeStruct(density.shape, jnp.float32),
         ),
-        in_specs=[vmem] * 8,
+        in_specs=[pl.BlockSpec(memory_space=pltpu.HBM)] * 8,
         out_specs=(vmem, vmem),
         scratch_shapes=[
             buffer(4, block_x + 4, block_y + 32, length_z),
             buffer(4, block_x + 5, block_y + 32, length_z),
             buffer(block_x + 1, block_y, length_z),
             buffer(block_x, block_y + 8, length_z),
-            pltpu.SemaphoreType.DMA((12,)),
-            pltpu.SemaphoreType.DMA((12,)),
+            pltpu.SemaphoreType.DMA((17,)),
+            pltpu.SemaphoreType.DMA((17,)),
             buffer(3, block_x, block_y, length_z),
             buffer(block_x, block_y, length_z),
             buffer(block_x, block_y, length_z),
@@ -740,20 +772,13 @@
             buffer(rows, full_x, lanes),
             pltpu.SemaphoreType.DMA((6, 2, count_x)),
             pltpu.SemaphoreType.DMA((2, count_y)),
+            *[pltpu.VMEM(value.shape, value.dtype) for value in operands],
+            pltpu.SemaphoreType.DMA((len(operands),)),
         ],
         compiler_params=pltpu.CompilerParams(
             collective_id=0, has_side_effects=True, vmem_limit_bytes=48 * 1024 * 1024
         ),
-    )(
-        velocity,
-        density,
-        jnp.asarray(table_z),
-        jnp.asarray(table_z.T.copy()),
-        jnp.asarray(table_x),
-        jnp.asarray(table_x.T.copy()),
-        decay,
-        gain,
-    )
+    )(*operands)
 
 
 def solution(mesh):

time: 72.2 us -> 69.7 us (0.965)
  Pallas kernels: 63.5 us -> 61 us
    pallas_call x1, Pallas kernels: 63.5 us -> 61 us  [per_device(): pl.pallas_call(functools.partial(step_kernel, count_x, count_y), out_shap...]
where the time goes in v4:
time: 69.7 us; the launch traced here: 69.3 us
  Pallas kernels  61 us (88%)
  local copies, waits for them, and re-layouts  7.43 us (11%)
    pallas_call x1, Pallas kernels, per_device(): pl.pallas_call(functools.partial(step_kernel, count_x, count_y), out_shap...  61 us
    unnamed x14, local copies, waits for them, and re-layouts  7.43 us

profile of v4, /device:TPU:0, one launch (start us, length us, event | category | flops | bytes accessed | tf_op | source)
XLA Modules:
  0.0 69.3 jit_solution(14056006673272283467)
XLA Ops:
  0.8 0.1 and_select_fusion
  0.9 0.0 copy-start
  0.9 1.1 %copy-done = bf16[3,16,32,256]{3,2,1,0:T(8,128)(2,1)S(1)} copy-done((bf16[3,16,32,256]{3,2,1,0:T(8,128)(2,1)S(1)}, bf16[3,16,32,256]{3,2,1,0:T(8,128)(2,1)}, u32[]{:S(2)}) %copy-start) | copy-done | bytes 786456
  2.0 0.0 copy-start.1
  2.0 0.9 %copy-done.1 = bf16[16,32,256]{2,1,0:T(8,128)(2,1)S(1)} copy-done((bf16[16,32,256]{2,1,0:T(8,128)(2,1)S(1)}, bf16[16,32,256]{2,1,0:T(8,128)(2,1)}, u32[]{:S(2)}) %copy-start.1) | copy-done | bytes 262168
  3.0 0.0 copy-start.2
  3.0 0.9 %copy-done.2 = f32[256,256]{1,0:T(8,128)S(1)} copy-done((f32[256,256]{1,0:T(8,128)S(1)}, f32[256,256]{1,0:T(8,128)}, u32[]{:S(2)}) %copy-start.2) | copy-done | bytes 262168
  3.9 0.0 copy-start.3
  3.9 0.9 %copy-done.3 = f32[256,256]{1,0:T(8,128)S(1)} copy-done((f32[256,256]{1,0:T(8,128)S(1)}, f32[256,256]{1,0:T(8,128)}, u32[]{:S(2)}) %copy-start.3) | copy-done | bytes 262168
  4.9 0.0 copy-start.4
  4.9 0.8 %copy-done.4 = f32[64,64]{1,0:T(8,128)S(1)} copy-done((f32[64,64]{1,0:T(8,128)S(1)}, f32[64,64]{1,0:T(8,128)}, u32[]{:S(2)}) %copy-start.4) | copy-done | bytes 16408
  5.6 0.0 copy-start.5
  5.6 0.8 %copy-done.5 = f32[64,64]{1,0:T(8,128)S(1)} copy-done((f32[64,64]{1,0:T(8,128)S(1)}, f32[64,64]{1,0:T(8,128)}, u32[]{:S(2)}) %copy-start.5) | copy-done | bytes 16408
  6.4 61.0 %shard_map.77 = (f32[3,16,32,256]{3,2,1,0:T(8,128)S(1)}, f32[16,32,256]{2,1,0:T(8,128)S(1)}) custom-call(bf16[3,16,32,256]{3,2,1,0:T(8,128)(2,1)S(1)} %copy-done, bf16[16,32,256]{2,1,0:T(8,128)(2,1)S(1)} %copy-done.1, f32[256,256]{1,0:T(8,128)S(1)} %copy-done.3, f32[256,256]{1,0:T(8,128)S(1)} %copy-done.2, f32[64,64]{1,0:T(8,128)S(1)} %copy-done.5, ...), custom_call_target="tpu_custom_call" | custom-call | tf_op jit(solution)/shard_map/pallas_call | solution.py:744
  67.4 1.1 %copy.10 = f32[3,16,32,256]{3,2,1,0:T(8,128)} copy(f32[3,16,32,256]{3,2,1,0:T(8,128)S(1)} %get-tuple-element.6) | data formatting | bytes 3145728
  68.5 0.8 %copy.11 = f32[16,32,256]{2,1,0:T(8,128)} copy(f32[16,32,256]{2,1,0:T(8,128)S(1)} %get-tuple-element.7) | data formatting | bytes 1048576
  (4 shorter events, 0.1 us)
Async XLA Ops:
  0.9 1.1 %copy-start = (bf16[3,16,32,256]{3,2,1,0:T(8,128)(2,1)S(1)}, bf16[3,16,32,256]{3,2,1,0:T(8,128)(2,1)}, u32[]{:S(2)}) copy-start(bf16[3,16,32,256]{3,2,1,0:T(8,128)(2,1)} %velocity_ref.1) | copy-start | bytes 2359300
  2.0 0.9 %copy-start.1 = (bf16[16,32,256]{2,1,0:T(8,128)(2,1)S(1)}, bf16[16,32,256]{2,1,0:T(8,128)(2,1)}, u32[]{:S(2)}) copy-start(bf16[16,32,256]{2,1,0:T(8,128)(2,1)} %density_ref.1) | copy-start | bytes 786436
  3.0 0.9 %copy-start.2 = (f32[256,256]{1,0:T(8,128)S(1)}, f32[256,256]{1,0:T(8,128)}, u32[]{:S(2)}) copy-start(f32[256,256]{1,0:T(8,128)} %constant.50.clone.tzt_ref) | copy-start | bytes 786436
  3.9 0.9 %copy-start.3 = (f32[256,256]{1,0:T(8,128)S(1)}, f32[256,256]{1,0:T(8,128)}, u32[]{:S(2)}) copy-start(f32[256,256]{1,0:T(8,128)} %constant.49.clone.tz_ref) | copy-start | bytes 786436
  4.9 0.8 %copy-start.4 = (f32[64,64]{1,0:T(8,128)S(1)}, f32[64,64]{1,0:T(8,128)}, u32[]{:S(2)}) copy-start(f32[64,64]{1,0:T(8,128)} %constant.52.clone.txt_ref) | copy-start | bytes 49156
  5.6 0.8 %copy-start.5 = (f32[64,64]{1,0:T(8,128)S(1)}, f32[64,64]{1,0:T(8,128)}, u32[]{:S(2)}) copy-start(f32[64,64]{1,0:T(8,128)} %constant.51.clone.tx_ref) | copy-start | bytes 49156

commit v5 on v4

--- a/solution.py
+++ b/solution.py
@@ -776,7 +776,7 @@
             pltpu.SemaphoreType.DMA((len(operands),)),
         ],
         compiler_params=pltpu.CompilerParams(
-            collective_id=0, has_side_effects=True, vmem_limit_bytes=48 * 1024 * 1024
+            collective_id=0, has_side_effects=True, vmem_limit_bytes=64 * 1024 * 1024
         ),
     )(*operands)
 

time: 69.7 us -> 67.1 us (0.963)
  local copies, waits for them, and re-layouts: 7.43 us -> 3.58 us
  Pallas kernels: 61 us -> 61.9 us
    unnamed x14 -> x4, local copies, waits for them, and re-layouts: 7.43 us -> 3.58 us
    pallas_call x1, Pallas kernels: 61 us -> 61.9 us  [per_device(): pl.pallas_call(functools.partial(step_kernel, count_x, count_y), out_shap...]
where the time goes in v5:
time: 67.1 us; the launch traced here: 67 us
  Pallas kernels  61.9 us (92%)
  local copies, waits for them, and re-layouts  3.58 us (5%)
  other arithmetic  0.84 us (1%)
    pallas_call x1, Pallas kernels, per_device(): pl.pallas_call(functools.partial(step_kernel, count_x, count_y), out_shap...  61.9 us
    unnamed x4, local copies, waits for them, and re-layouts  3.58 us

profile of v5, /device:TPU:0, one launch (start us, length us, event | category | flops | bytes accessed | tf_op | source)
XLA Modules:
  0.0 67.0 jit_solution(246136729432580735)
XLA Ops:
  0.8 0.7 %and_select_fusion = (f32[64,128]{1,0:T(8,128)}, f32[64,128]{1,0:T(8,128)}) fusion(f32[128]{0:T(128)S(1)} %sine_multiply_fusion, f32[64]{0:T(128)S(1)} %sine_multiply_fusion.1, pred[128]{0:T(512)(128)(4,1)S(1)} %broadcast_compare_fusion, pred[64]{0:T(512)(128)(4,1)S(1)} %iota_compare_fusion), kind=kLoop, calls=%fused_computation.4 | loop fusion | flops 98304 | bytes 66496 | tf_op jit(solution)/shard_map/jit(_where)/select_n | solution.py:297
  1.5 61.9 %shard_map.77 = (f32[3,16,32,256]{3,2,1,0:T(8,128)}, f32[16,32,256]{2,1,0:T(8,128)}) custom-call(bf16[3,16,32,256]{3,2,1,0:T(8,128)(2,1)} %velocity_ref.1, bf16[16,32,256]{2,1,0:T(8,128)(2,1)} %density_ref.1, f32[256,256]{1,0:T(8,128)} %constant.49.clone.tz_ref, f32[256,256]{1,0:T(8,128)} %constant.50.clone.tzt_ref, f32[64,64]{1,0:T(8,128)} %constant.51.clone.tx_ref, ...), custom_call_target="tpu_custom_call" | custom-call | tf_op jit(solution)/shard_map/pallas_call | solution.py:744
  63.4 0.0 copy-start
  63.4 2.8 %copy.10 = f32[3,16,32,256]{3,2,1,0:T(8,128)} copy(f32[3,16,32,256]{3,2,1,0:T(8,128)} %get-tuple-element.6) | data formatting | bytes 3145728
  66.2 0.0 copy-done
  66.2 0.8 %copy.11 = f32[16,32,256]{2,1,0:T(8,128)} copy(f32[16,32,256]{2,1,0:T(8,128)S(1)} %copy-done) | data formatting | bytes 1048576
  (4 shorter events, 0.1 us)
Async XLA Ops:
  63.4 2.8 %copy-start = (f32[16,32,256]{2,1,0:T(8,128)S(1)}, f32[16,32,256]{2,1,0:T(8,128)}, u32[]{:S(2)}) copy-start(f32[16,32,256]{2,1,0:T(8,128)} %get-tuple-element.7) | copy-start | bytes 1572868
